TPU v7x, 32 devices: a whole 2x2x4 slice. The times are simulated.
32 devices in a mesh: wide: 8 (over z, y), narrow: 4 (over x, core).
Axes of the slice: x: 2, y: 2, z: 4, core: 2. Of those that a mesh axis runs over, the one named last changes fastest.
Arguments:
- occupied: bfloat16 [64, 64, 4096], P('wide', 'narrow'), may hold values from -6 to 6
- empty: bfloat16 [128, 64, 4096], P('wide', 'narrow'), may hold values from -6 to 6
- pair_occ: int32 [256], P('wide'), may hold values from 0 to 7
- pair_emp: int32 [256], P('wide'), may hold values from 0 to 15
- pair_level: int32 [256], replicated, may hold values from 0 to 63
- denominators: float32 [64, 8], replicated, may hold values from 0.02 to 0.2
- trial: bfloat16 [131072, 512], P(('wide', 'narrow')), may hold values from -0.015625 to 0.015625
Outputs:
- response: bfloat16 [8, 131072, 512], P(None, ('wide', 'narrow'))
Inputs may be any that keep to these rules, and one draw needn't show every extreme that they name: Pair p uses occupied band (p // 32) * 8 + pair_occ[p]. Pair p uses empty band (p // 32) * 16 + pair_emp[p].
All inputs are finite; a program needn't handle non-finite values.
Results may differ from a plain program's by a relative error of at most 0.012.
Values may be sent and summed in bfloat16 or wider, within the bound.
No kernel may reach another device: no remote copies, remote signals or barrier semaphores. Data moves between devices by JAX's collectives and lax.ppermute only.
A program may use at most 128 MiB of HBM per device.

v0:
```python
import functools
import math

import jax
import jax.numpy as jnp
import numpy as np
from jax import lax
from jax.experimental import pallas as pl
from jax.experimental.pallas import tpu as pltpu
from jax.sharding import PartitionSpec as P

GROUP = 16
LANES = 128
SPLITS = ((1, 1), (1,))
PERMUTE_MOST = 8
VMEM = 56 * 1024 * 1024
F32 = jnp.float32
BF16 = jnp.bfloat16


def rounded(values):
    return np.asarray(values, np.float32).astype(jnp.bfloat16)


def tables(grid, slabs):
    scaling = np.float32(1.0 / math.sqrt(grid))
    step = np.float32(2.0 * math.pi / grid)
    at = np.arange(grid)
    half = np.arange(grid // 2)

    def cos_sin(a, b):
        angle = (a[:, None] * b[None, :] % grid).astype(np.float32) * step
        return (
            rounded(np.cos(angle) * scaling).astype(np.float32),
            rounded(np.sin(angle) * scaling).astype(np.float32),
        )

    planes = grid // slabs
    depth = grid // 2 // slabs
    channels = 2 * depth
    group = LANES // channels
    zc, zs = cos_sin(at, half)
    ztab = np.stack([zc, -zs], -1).reshape(grid, slabs, channels)
    zmat = np.einsum("ab,znq->aznbq", np.eye(group, dtype=np.float32), ztab)
    zmat = zmat.reshape(group * grid, slabs * group * channels)
    signed = np.where(half < grid // 4, half, half - grid // 2)
    yc, ys = cos_sin(signed, at)
    mix = np.zeros((grid, 2, grid // 2, 2), np.float32)
    mix[:, 0, :, 0] = yc.T
    mix[:, 1, :, 0] = ys.T
    mix[:, 0, :, 1] = -ys.T
    mix[:, 1, :, 1] = yc.T
    ymat = np.einsum("yajb,dk->ydajkb", mix, np.eye(depth, dtype=np.float32))
    ymat = ymat.reshape(grid * channels, grid // 2 * channels)
    xc, xs = cos_sin(at, at)
    xtab = np.stack([xc, xs]).reshape(2, grid, slabs, planes)
    xmat = np.einsum("hksx,pr->skphrx", xtab, np.eye(8, dtype=np.float32))
    xmat = xmat.reshape(slabs, grid * 8, 2 * 8 * planes)
    swap = np.zeros((2 * LANES, 2 * LANES), np.float32)
    even = np.arange(0, 2 * LANES, 2)
    swap[even + 1, even] = 1.0
    swap[even, even + 1] = -1.0
    return rounded(zmat), rounded(ymat), rounded(xmat), rounded(swap)


def front_kernel(start, slabs, widths, occ_at, emp_at, places, occ, emp, zmat, ymat, *rest):
    outs, (prod, lines) = rest[:-2], rest[-2:]
    planes = occ.shape[1]
    width = zmat.shape[0]
    steps = occ.shape[2] // width
    for p in range(GROUP):
        o, e = occ_at[start + p], emp_at[start + p]
        row = (occ[o].astype(F32) * emp[e].astype(F32)).astype(BF16)
        for g in range(steps):
            prod[g, p * planes : (p + 1) * planes, :] = row[:, g * width : (g + 1) * width]
    for g in range(steps):
        along = jnp.dot(prod[g], zmat[...], preferred_element_type=F32).astype(BF16)
        for n in range(slabs):
            lines[n, :, g * LANES : (g + 1) * LANES] = along[:, n * LANES : (n + 1) * LANES]
    for s in range(slabs):
        along = jnp.dot(lines[places[s]], ymat[...], preferred_element_type=F32).astype(BF16)
        first = 0
        for h, wide in enumerate(widths):
            outs[h * slabs + s][...] = along[:, first : first + wide]
            first += wide


def front(start, slabs, widths, occ_at, emp_at, places, occ, emp, zmat, ymat):
    rows = GROUP * occ.shape[1]
    width = zmat.shape[0]
    steps = occ.shape[2] // width
    smem = pl.BlockSpec(memory_space=pltpu.SMEM)
    vmem = pl.BlockSpec(memory_space=pltpu.VMEM)
    flops = 2 * rows * (steps * width * zmat.shape[1] + slabs * ymat.shape[0] * ymat.shape[1])
    outs = pl.pallas_call(
        functools.partial(front_kernel, start, slabs, widths),
        out_shape=[jax.ShapeDtypeStruct((rows, w), BF16) for w in widths for _ in range(slabs)],
        in_specs=[smem] * 3 + [vmem] * 4,
        out_specs=[vmem] * (len(widths) * slabs),
        scratch_shapes=[
            pltpu.VMEM((steps, rows, width), BF16),
            pltpu.VMEM((slabs, rows, ymat.shape[0]), BF16),
        ],
        compiler_params=pltpu.CompilerParams(vmem_limit_bytes=VMEM),
        cost_estimate=pl.CostEstimate(
            flops=flops, bytes_accessed=2 * (occ.size + emp.size), transcendentals=0
        ),
        name="front",
    )(occ_at, emp_at, places, occ, emp, zmat, ymat)
    return [outs[h * slabs : (h + 1) * slabs] for h in range(len(widths))]


def across_kernel(slabs, blocks, first, grid, places, *rest):
    parts, (xmat, swap), outs, whole = (
        rest[:slabs],
        rest[slabs : slabs + 2],
        rest[slabs + 2 : -1],
        rest[-1],
    )
    wide = parts[0].shape[1]
    planes = parts[0].shape[0] // GROUP
    half = grid // 2
    channels = 2 * (half // slabs)
    lane = first + lax.broadcasted_iota(jnp.int32, (grid, wide), 1)
    kx = lax.broadcasted_iota(jnp.int32, (grid, wide), 0)
    kx = jnp.where(kx < half, kx, kx - grid)
    ky = lane // channels
    ky = jnp.where(ky < half // 2, ky, ky - half)
    kz = places[0] * (channels // 2) + lane % channels // 2
    squared = (kx * kx + ky * ky + kz * kz).astype(F32)
    quarter = float(grid // 4)
    coulomb = (1.0 / jnp.sqrt(1.0 + squared / (quarter * quarter)))[:, None, :]
    left = jnp.concatenate([xmat[places[s]] for s in range(slabs)], axis=1)
    found = []
    for m in range(GROUP // 8):
        right = []
        for s in range(slabs):
            plain = parts[s][m * 8 * planes : (m + 1) * 8 * planes, :]
            right.append(plain)
            turned = [
                jnp.dot(plain[:, c : c + 2 * LANES], swap[...], preferred_element_type=F32)
                for c in range(0, wide, 2 * LANES)
            ]
            right.append(jnp.concatenate(turned, axis=1).astype(BF16))
        right = jnp.concatenate(right, axis=0)
        total = jnp.dot(left, right, preferred_element_type=F32)
        found.append(total.reshape(grid, 8, wide) * coulomb)
    found = jnp.concatenate(found, axis=1).astype(BF16)
    whole[...] = found.reshape(whole.shape)
    for s in range(blocks):
        outs[s][...] = whole[places[slabs + s]]


def across(slabs, blocks, first, grid, places, parts, xmat, swap):
    rows, wide = parts[0].shape
    tall = grid // blocks * GROUP
    smem = pl.BlockSpec(memory_space=pltpu.SMEM)
    vmem = pl.BlockSpec(memory_space=pltpu.VMEM)
    flops = 2 * GROUP // 8 * xmat.shape[1] * xmat.shape[2] * slabs * wide
    return pl.pallas_call(
        functools.partial(across_kernel, slabs, blocks, first, grid),
        out_shape=[jax.ShapeDtypeStruct((tall, wide), BF16)] * blocks,
        in_specs=[smem] + [vmem] * (slabs + 2),
        out_specs=[vmem] * blocks,
        scratch_shapes=[pltpu.VMEM((blocks, tall, wide), BF16)],
        compiler_params=pltpu.CompilerParams(vmem_limit_bytes=VMEM),
        cost_estimate=pl.CostEstimate(
            flops=flops, bytes_accessed=4 * slabs * rows * wide, transcendentals=0
        ),
        name="across",
    )(places, *parts, xmat, swap)


def project_kernel(blocks, slabs, widths, places, trial, *rest):
    parts, (shares, turned) = rest[:-2], rest[-2:]
    count = blocks * len(widths)
    parts = parts[:count]
    lanes = sum(widths)
    heights = parts[0].shape[0] // GROUP
    total = jnp.zeros((blocks * GROUP, trial.shape[1]), F32)
    for x in range(heights):
        first = x * lanes
        for h, wide in enumerate(widths):
            left = jnp.concatenate(
                [parts[h * blocks + s][x * GROUP : (x + 1) * GROUP, :] for s in range(blocks)], axis=0
            )
            total += jnp.dot(left, trial[first : first + wide, :], preferred_element_type=F32)
            turned[first : first + wide, :] = left.T
            first += wide
    step = trial.shape[1] // slabs
    for s in range(blocks):
        for n in range(slabs):
            shares[places[slabs + s] * slabs + n] = total[
                s * GROUP : (s + 1) * GROUP, n * step : (n + 1) * step
            ].astype(shares.dtype)


def project(blocks, slabs, widths, places, trial, parts):
    columns, vectors = trial.shape
    pairs = blocks * GROUP
    smem = pl.BlockSpec(memory_space=pltpu.SMEM)
    vmem = pl.BlockSpec(memory_space=pltpu.VMEM)
    return pl.pallas_call(
        functools.partial(project_kernel, blocks, slabs, widths),
        out_shape=[
            jax.ShapeDtypeStruct((blocks * slabs, GROUP, vectors // slabs), BF16),
            jax.ShapeDtypeStruct((columns, pairs), BF16),
        ],
        in_specs=[smem] + [vmem] * (1 + len(parts)),
        out_specs=[vmem] * 2,
        compiler_params=pltpu.CompilerParams(vmem_limit_bytes=VMEM),
        cost_estimate=pl.CostEstimate(
            flops=2 * pairs * columns * vectors,
            bytes_accessed=2 * columns * (vectors + 2 * pairs),
            transcendentals=0,
        ),
        name="project",
    )(places, trial, *parts)


def respond_kernel(blocks, slabs, groups, freqs, places, *rest):
    shares = rest[:groups]
    weights = rest[groups : 2 * groups]
    turned = rest[2 * groups : 3 * groups]
    out, weighted = rest[3 * groups :]
    vectors = out.shape[2]
    step = vectors // slabs

    @pl.when(pl.program_id(0) == 0)
    def _():
        for g in range(groups):
            for s in range(blocks):
                source = places[slabs + s]
                row = (g * blocks + s) * GROUP
                scale = weights[g][source]
                for n in range(slabs):
                    share = shares[g][source * slabs + n].astype(F32)
                    for w in range(freqs):
                        weighted[w, row : row + GROUP, n * step : (n + 1) * step] = (
                            scale[:, w : w + 1] * share
                        ).astype(BF16)

    left = jnp.concatenate([t[...] for t in turned], axis=1)
    for w in range(freqs):
        out[w] = jnp.dot(left, weighted[w], preferred_element_type=F32).astype(BF16)


def respond(blocks, slabs, places, shares, weights, turned, vectors):
    groups = len(shares)
    columns, pairs = turned[0].shape
    freqs = weights[0].shape[2]
    height = min(columns, 256)
    smem = pl.BlockSpec(memory_space=pltpu.SMEM)
    vmem = pl.BlockSpec(memory_space=pltpu.VMEM)
    return pl.pallas_call(
        functools.partial(respond_kernel, blocks, slabs, groups, freqs),
        grid=(columns // height,),
        out_shape=jax.ShapeDtypeStruct((freqs, columns, vectors), BF16),
        in_specs=[smem]
        + [vmem] * (2 * groups)
        + [pl.BlockSpec((height, pairs), lambda i: (i, 0))] * groups,
        out_specs=pl.BlockSpec((freqs, height, vectors), lambda i: (0, i, 0)),
        scratch_shapes=[pltpu.VMEM((freqs, groups * pairs, vectors), BF16)],
        compiler_params=pltpu.CompilerParams(vmem_limit_bytes=VMEM),
        cost_estimate=pl.CostEstimate(
            flops=2 * groups * pairs * columns * vectors * freqs,
            bytes_accessed=2 * freqs * columns * vectors,
            transcendentals=0,
        ),
        name="respond",
    )(places, *shares, *weights, *turned)


def exchange(blocks, axis):
    size = len(blocks)
    if size > PERMUTE_MOST:
        return list(lax.all_to_all(jnp.stack(blocks), axis, 0, 0, tiled=True))
    return [blocks[0]] + [
        lax.ppermute(blocks[s], axis, [(i, i ^ s) for i in range(size)]) for s in range(1, size)
    ]


def partners(axis):
    size = lax.axis_size(axis)
    steps = jnp.arange(size, dtype=jnp.int32)
    return steps if size > PERMUTE_MOST else lax.axis_index(axis) ^ steps


def sum_shares(shares):
    both = ("wide", "narrow")
    count = shares.shape[0]
    taken = lax.all_to_all(shares, both, 0, 0, tiled=True)
    total = jnp.sum(taken.astype(F32), axis=0, keepdims=True)
    spread = jnp.broadcast_to(total, (count,) + total.shape[1:])
    return lax.all_to_all(spread, both, 0, 0, tiled=True)


def shards(occupied, empty, pair_occ, pair_emp, pair_level, denominators, trial):
    slabs = lax.axis_size("narrow")
    blocks = lax.axis_size("wide")
    grid = occupied.shape[1] * slabs
    zmat, ymat, xmat, swap = (jnp.asarray(t) for t in tables(grid, slabs))
    places = jnp.concatenate([partners("narrow"), partners("wide")])
    lanes = ymat.shape[1]
    groups = pair_occ.shape[0] // GROUP
    vectors = trial.shape[1]
    levels = jnp.arange(denominators.shape[0], dtype=jnp.int32)
    onehot = (pair_level[:, None] == levels[None, :]).astype(F32)
    weights = jnp.dot(onehot, denominators, precision=lax.Precision.HIGHEST)
    weights = weights.reshape(blocks, groups, GROUP, -1)

    shares, turned = [], []
    for g in range(groups):
        cut = SPLITS[g % len(SPLITS)]
        widths = tuple(lanes * c // sum(cut) for c in cut)
        sent = front(
            g * GROUP, slabs, widths, pair_occ, pair_emp, places, occupied, empty, zmat, ymat
        )
        parts, first = [], 0
        for h, wide in enumerate(widths):
            got = exchange(sent[h], "narrow")
            waves = across(slabs, blocks, first, grid, places, got, xmat, swap)
            parts += exchange(waves, "wide")
            first += wide
        share, turn = project(blocks, slabs, widths, places, trial, parts)
        shares.append(sum_shares(share))
        turned.append(turn)
    return respond(
        blocks,
        slabs,
        places,
        shares,
        [weights[:, g] for g in range(groups)],
        turned,
        vectors,
    )


def solution(mesh):
    placed = (
        P("wide", "narrow", None),
        P("wide", "narrow", None),
        P("wide"),
        P("wide"),
        P(),
        P(),
        P(("wide", "narrow"), None),
    )
    return jax.shard_map(
        shards,
        mesh=mesh,
        in_specs=placed,
        out_specs=P(None, ("wide", "narrow"), None),
        check_vma=False,
    )
```

profile of v0, /device:TPU:0, one launch (start us, length us, event | category | flops | bytes accessed | tf_op | source)
XLA Modules:
  0.0 170.7 jit_solution(5086773595463855155)
XLA Ops:
  0.0 0.7 pad_add_fusion.places
  0.7 5.8 %front.2 = (bf16[256,256]{1,0:T(8,128)(2,1)}, bf16[256,256]{1,0:T(8,128)(2,1)}, bf16[256,256]{1,0:T(8,128)(2,1)}, bf16[256,256]{1,0:T(8,128)(2,1)}, bf16[256,256...) custom-call(s32[32]{0:T(128)} %occ_at.3, s32[32]{0:T(128)} %emp_at.3, ...), custom_call_target="tpu_custom_call" | custom-call | flops 2147483648 | bytes 3145728 | tf_op jit(solution)/shard_map/front/pallas_call | solution.py:95
  7.0 2.5 %collective-permute-start.1 = (bf16[256,256]{1,0:T(8,128)(2,1)}, bf16[256,256]{1,0:T(8,128)(2,1)S(1)}, u32[]{:S(2)}, u32[]{:S(2)}) collective-permute-start(bf16[256,256]{1,0:T(8,128)(2,1)} %get-tuple-element.47), channel_id=1, source_target_pairs={{0,2},{1,3},{2,0},{3,1},{4,6},{5,7},{6,4},{7,5},{8,10},{9,11},{10,... | collective-permute-start | bytes 393224 | tf_op jit(solution)/shard_map/ppermute | solution.py:279
  9.7 1.9 %collective-permute-start.11 = (bf16[256,256]{1,0:T(8,128)(2,1)}, bf16[256,256]{1,0:T(8,128)(2,1)S(1)}, u32[]{:S(2)}, u32[]{:S(2)}) collective-permute-start(bf16[256,256]{1,0:T(8,128)(2,1)} %get-tuple-element.59), channel_id=1, source_target_pairs={{0,2},{1,3},{2,0},{3,1},{4,6},{5,7},{6,4},{7,5},{8,10},{9,11},{10,... | collective-permute-start | bytes 393224 | tf_op jit(solution)/shard_map/ppermute | solution.py:279
  11.6 2.4 %collective-permute-done.1.rest_2_ = bf16[256,256]{1,0:T(8,128)(2,1)S(1)} collective-permute-done((bf16[256,256]{1,0:T(8,128)(2,1)}, bf16[256,256]{1,0:T(8,128)(2,1)S(1)}, u32[]{:S(2)}, u32[]{:S(2)}) %collective-permute-start.1) | collective-permute-done | bytes 131104 | tf_op jit(solution)/shard_map/ppermute | solution.py:279
  14.1 2.4 %collective-permute-done.2.rest_3_ = bf16[256,256]{1,0:T(8,128)(2,1)S(1)} collective-permute-done((bf16[256,256]{1,0:T(8,128)(2,1)}, bf16[256,256]{1,0:T(8,128)(2,1)S(1)}, u32[]{:S(2)}, u32[]{:S(2)}) %collective-permute-start.2) | collective-permute-done | bytes 131104 | tf_op jit(solution)/shard_map/ppermute | solution.py:279
  17.1 3.3 %across.3 = (bf16[128,256]{1,0:T(8,128)(2,1)}, bf16[128,256]{1,0:T(8,128)(2,1)}, bf16[128,256]{1,0:T(8,128)(2,1)}, bf16[128,256]{1,0:T(8,128)(2,1)}, bf16[128,25...) custom-call(s32[12]{0:T(128)} %pad_add_fusion.places, ...), custom_call_target="tpu_custom_call" | custom-call | flops 536870912 | bytes 1048576 | tf_op jit(solution)/shard_map/across/pallas_call | solution.py:160
  20.4 1.6 collective-permute-start.3
  22.0 1.6 collective-permute-start.4
  24.0 5.8 %front.3 = (bf16[256,512]{1,0:T(8,128)(2,1)}, bf16[256,512]{1,0:T(8,128)(2,1)}, bf16[256,512]{1,0:T(8,128)(2,1)}, bf16[256,512]{1,0:T(8,128)(2,1)}) custom-call(s32[32]{0:T(128)} %occ_at.3, s32[32]{0:T(128)} %emp_at.3, s32[12]{0:T(128)} %pad_add_fusion.places, bf16[8,16,4096]{2,1,0:T(8,128)(2,1)} %occ.3, bf16[16,16,4096]{2,1,0:T(8,128)(2,1)} %emp.3, ...), custom_call_target="tpu_custom_call" | custom-call | flops 2147483648 | bytes 3145728 | tf_op jit(solution)/shard_map/front/pallas_call | solution.py:95
  29.9 1.5 collective-permute-start.21
  31.7 2.7 %collective-permute-start.6 = (bf16[128,256]{1,0:T(8,128)(2,1)S(1)}, bf16[128,256]{1,0:T(8,128)(2,1)S(1)}, u32[]{:S(2)}, u32[]{:S(2)}) collective-permute-start(bf16[128,256]{1,0:T(8,128)(2,1)S(1)} %copy-done.41), channel_id=1, source_target_pairs={{0,16},{4,20},{8,24},{12,28},{16,0},{20,4},{24,8},{28,12},{1,17},{... | collective-permute-start | bytes 196616 | tf_op jit(solution)/shard_map/ppermute | solution.py:279
  34.4 1.4 collective-permute-start.7
  35.8 2.7 %collective-permute-done.6.rest_4_ = bf16[128,256]{1,0:T(8,128)(2,1)S(1)} collective-permute-done((bf16[128,256]{1,0:T(8,128)(2,1)S(1)}, bf16[128,256]{1,0:T(8,128)(2,1)S(1)}, u32[]{:S(2)}, u32[]{:S(2)}) %collective-permute-start.6) | collective-permute-done | bytes 65568 | tf_op jit(solution)/shard_map/ppermute | solution.py:279
  38.5 5.0 %collective-permute-start.8 = (bf16[128,256]{1,0:T(8,128)(2,1)S(1)}, bf16[128,256]{1,0:T(8,128)(2,1)S(1)}, u32[]{:S(2)}, u32[]{:S(2)}) collective-permute-start(bf16[128,256]{1,0:T(8,128)(2,1)S(1)} %copy-done.39), channel_id=1, source_target_pairs={{0,24},{4,28},{8,16},{12,20},{16,8},{20,12},{24,0},{28,4},{1,25},{... | collective-permute-start | bytes 196616 | tf_op jit(solution)/shard_map/ppermute | solution.py:279
  43.4 2.3 %collective-permute-start.9 = (bf16[128,256]{1,0:T(8,128)(2,1)S(1)}, bf16[128,256]{1,0:T(8,128)(2,1)S(1)}, u32[]{:S(2)}, u32[]{:S(2)}) collective-permute-start(bf16[128,256]{1,0:T(8,128)(2,1)S(1)} %copy-done.38), channel_id=1, source_target_pairs={{0,28},{4,24},{8,20},{12,16},{16,12},{20,8},{24,4},{28,0},{1,29},{... | collective-permute-start | bytes 196616 | tf_op jit(solution)/shard_map/ppermute | solution.py:279
  45.7 3.2 %across.4 = (bf16[128,256]{1,0:T(8,128)(2,1)}, bf16[128,256]{1,0:T(8,128)(2,1)}, bf16[128,256]{1,0:T(8,128)(2,1)}, bf16[128,256]{1,0:T(8,128)(2,1)}, bf16[128,25...) custom-call(s32[12]{0:T(128)} %pad_add_fusion.places, ...), custom_call_target="tpu_custom_call" | custom-call | flops 536870912 | bytes 1048576 | tf_op jit(solution)/shard_map/across/pallas_call | solution.py:160
  49.0 1.6 collective-permute-start.13
  50.6 3.0 %collective-permute-done.13.rest_9_ = bf16[128,256]{1,0:T(8,128)(2,1)S(1)} collective-permute-done((bf16[128,256]{1,0:T(8,128)(2,1)}, bf16[128,256]{1,0:T(8,128)(2,1)S(1)}, u32[]{:S(2)}, u32[]{:S(2)}) %collective-permute-start.13) | collective-permute-done | bytes 65568 | tf_op jit(solution)/shard_map/ppermute | solution.py:279
  53.5 1.5 collective-permute-done.14.rest_10_
  55.0 1.5 collective-permute-start.16
  56.6 2.3 %collective-permute-start.17 = (bf16[128,256]{1,0:T(8,128)(2,1)}, bf16[128,256]{1,0:T(8,128)(2,1)S(1)}, u32[]{:S(2)}, u32[]{:S(2)}) collective-permute-start(bf16[128,256]{1,0:T(8,128)(2,1)} %get-tuple-element.66), channel_id=1, source_target_pairs={{0,20},{4,16},{8,28},{12,24},{16,4},{20,0},{24,12},{28,8},{1,21},{... | collective-permute-start | bytes 196616 | tf_op jit(solution)/shard_map/ppermute | solution.py:279
  58.9 1.5 collective-permute-start.18
  60.5 2.2 %collective-permute-start.19 = (bf16[128,256]{1,0:T(8,128)(2,1)}, bf16[128,256]{1,0:T(8,128)(2,1)S(1)}, u32[]{:S(2)}, u32[]{:S(2)}) collective-permute-start(bf16[128,256]{1,0:T(8,128)(2,1)} %get-tuple-element.68), channel_id=1, source_target_pairs={{0,28},{4,24},{8,20},{12,16},{16,12},{20,8},{24,4},{28,0},{1,29},{... | collective-permute-start | bytes 196616 | tf_op jit(solution)/shard_map/ppermute | solution.py:279
  62.7 4.1 %across.5 = (bf16[128,512]{1,0:T(8,128)(2,1)}, bf16[128,512]{1,0:T(8,128)(2,1)}, bf16[128,512]{1,0:T(8,128)(2,1)}, bf16[128,512]{1,0:T(8,128)(2,1)}, bf16[128,51...) custom-call(s32[12]{0:T(128)} %pad_add_fusion.places, ...), custom_call_target="tpu_custom_call" | custom-call | flops 1073741824 | bytes 2097152 | tf_op jit(solution)/shard_map/across/pallas_call | solution.py:160
  66.9 1.6 collective-permute-start.23
  69.2 4.3 %project.2 = (bf16[32,16,128]{2,1,0:T(8,128)(2,1)}, bf16[4096,128]{1,0:T(8,128)(2,1)}) custom-call(s32[12]{0:T(128)} %pad_add_fusion.places, bf16[4096,512]{1,0:T(8,128)(2,1)} %trial.3, bf16[128,256]{1,0:T(8,128)(2,1)} %get-tuple-element.49.rest_0_, bf16[128,256]{1,0:T(8,128)(2,1)} %copy-done.10, bf16[128,256]{1,0:T(8,128)(2,1)} %copy-done.11, ...), custom_call_target="tpu_custom_call" | custom-call | flops 536870912 | bytes 6291456 | tf_op jit(solution)/shard_map/project/pallas_call | solution.py:203
  73.5 4.1 %all-to-all-start = ((bf16[32,16,128]{2,1,0:T(8,128)(2,1)}), bf16[32,16,128]{2,1,0:T(8,128)(2,1)S(1)}, u32[]{:S(2)}, u32[]{:S(2)}) async-start(bf16[32,16,128]{2,1,0:T(8,128)(2,1)} %get-tuple-element.69), calls=%async_computation | async-start | bytes 262144 | tf_op jit(solution)/shard_map/all_to_all | solution.py:292
  77.6 2.7 %collective-permute-start.25 = (bf16[128,512]{1,0:T(8,128)(2,1)S(1)}, bf16[128,512]{1,0:T(8,128)(2,1)S(1)}, u32[]{:S(2)}, u32[]{:S(2)}) collective-permute-start(bf16[128,512]{1,0:T(8,128)(2,1)S(1)} %copy-done.34), channel_id=1, source_target_pairs={{0,12},{4,8},{8,4},{12,0},{16,28},{20,24},{24,20},{28,16},{1,13},{... | collective-permute-start | bytes 393224 | tf_op jit(solution)/shard_map/ppermute | solution.py:279
  80.3 2.4 %collective-permute-start.26 = (bf16[128,512]{1,0:T(8,128)(2,1)S(1)}, bf16[128,512]{1,0:T(8,128)(2,1)S(1)}, u32[]{:S(2)}, u32[]{:S(2)}) collective-permute-start(bf16[128,512]{1,0:T(8,128)(2,1)S(1)} %copy-done.33), channel_id=1, source_target_pairs={{0,16},{4,20},{8,24},{12,28},{16,0},{20,4},{24,8},{28,12},{1,17},{... | collective-permute-start | bytes 393224 | tf_op jit(solution)/shard_map/ppermute | solution.py:279
  83.3 2.4 %collective-permute-start.28 = (bf16[128,512]{1,0:T(8,128)(2,1)S(1)}, bf16[128,512]{1,0:T(8,128)(2,1)S(1)}, u32[]{:S(2)}, u32[]{:S(2)}) collective-permute-start(bf16[128,512]{1,0:T(8,128)(2,1)S(1)} %copy-done.31), channel_id=1, source_target_pairs={{0,24},{4,28},{8,16},{12,20},{16,8},{20,12},{24,0},{28,4},{1,25},{... | collective-permute-start | bytes 393224 | tf_op jit(solution)/shard_map/ppermute | solution.py:279
  85.7 2.4 %collective-permute-start.29 = (bf16[128,512]{1,0:T(8,128)(2,1)S(1)}, bf16[128,512]{1,0:T(8,128)(2,1)S(1)}, u32[]{:S(2)}, u32[]{:S(2)}) collective-permute-start(bf16[128,512]{1,0:T(8,128)(2,1)S(1)} %copy-done.30), channel_id=1, source_target_pairs={{0,28},{4,24},{8,20},{12,16},{16,12},{20,8},{24,4},{28,0},{1,29},{... | collective-permute-start | bytes 393224 | tf_op jit(solution)/shard_map/ppermute | solution.py:279
  88.1 1.4 collective-permute-done.25.rest_3_
  89.5 9.4 %collective-permute-done.26.rest_4_ = bf16[128,512]{1,0:T(8,128)(2,1)S(1)} collective-permute-done((bf16[128,512]{1,0:T(8,128)(2,1)S(1)}, bf16[128,512]{1,0:T(8,128)(2,1)S(1)}, u32[]{:S(2)}, u32[]{:S(2)}) %collective-permute-start.26) | collective-permute-done | bytes 131104 | tf_op jit(solution)/shard_map/ppermute | solution.py:279
  98.9 3.3 %collective-permute-done.27.rest_5_ = bf16[128,512]{1,0:T(8,128)(2,1)S(1)} collective-permute-done((bf16[128,512]{1,0:T(8,128)(2,1)S(1)}, bf16[128,512]{1,0:T(8,128)(2,1)S(1)}, u32[]{:S(2)}, u32[]{:S(2)}) %collective-permute-start.27) | collective-permute-done | bytes 131104 | tf_op jit(solution)/shard_map/ppermute | solution.py:279
  103.0 4.3 %project.3 = (bf16[32,16,128]{2,1,0:T(8,128)(2,1)}, bf16[4096,128]{1,0:T(8,128)(2,1)}) custom-call(s32[12]{0:T(128)} %pad_add_fusion.places, bf16[4096,512]{1,0:T(8,128)(2,1)} %trial.3, bf16[128,512]{1,0:T(8,128)(2,1)} %get-tuple-element.74.rest_0_, bf16[128,512]{1,0:T(8,128)(2,1)} %copy-done.3, bf16[128,512]{1,0:T(8,128)(2,1)} %copy-done.4, ...), custom_call_target="tpu_custom_call" | custom-call | flops 536870912 | bytes 6291456 | tf_op jit(solution)/shard_map/project/pallas_call | solution.py:203
  107.3 7.6 %all-to-all-start.2 = ((bf16[32,16,128]{2,1,0:T(8,128)(2,1)}), bf16[32,16,128]{2,1,0:T(8,128)(2,1)S(1)}, u32[]{:S(2)}, u32[]{:S(2)}) async-start(bf16[32,16,128]{2,1,0:T(8,128)(2,1)} %get-tuple-element.82), calls=%async_computation.2 | async-start | bytes 262144 | tf_op jit(solution)/shard_map/all_to_all | solution.py:292
  114.9 8.2 %all-to-all-done.2 = bf16[32,16,128]{2,1,0:T(8,128)(2,1)S(1)} async-done(((bf16[32,16,128]{2,1,0:T(8,128)(2,1)}), bf16[32,16,128]{2,1,0:T(8,128)(2,1)S(1)}, u32[]{:S(2)}, u32[]{:S(2)}) %all-to-all-start.2) | async-done | bytes 131104 | tf_op jit(solution)/shard_map/all_to_all | solution.py:292
  123.1 0.7 broadcast_in_dim.4
  123.8 2.6 %all-to-all-start.1 = ((f32[32,16,128]{2,1,0:T(8,128)}), f32[32,16,128]{2,1,0:T(8,128)S(1)}, u32[]{:S(2)}, u32[]{:S(2)}) async-start(f32[32,16,128]{2,1,0:T(8,128)} %broadcast_in_dim.4), calls=%async_computation.1 | async-start | bytes 524288 | tf_op jit(solution)/shard_map/all_to_all | solution.py:295
  126.4 10.6 %all-to-all-done.1.rest_0_ = f32[32,16,128]{2,1,0:T(8,128)S(1)} async-done(((f32[32,16,128]{2,1,0:T(8,128)}), f32[32,16,128]{2,1,0:T(8,128)S(1)}, u32[]{:S(2)}, u32[]{:S(2)}) %all-to-all-start.1) | async-done | bytes 262176 | tf_op jit(solution)/shard_map/all_to_all | solution.py:295
  137.0 0.7 broadcast_in_dim.5
  137.7 2.6 %all-to-all-start.3 = ((f32[32,16,128]{2,1,0:T(8,128)}), f32[32,16,128]{2,1,0:T(8,128)S(1)}, u32[]{:S(2)}, u32[]{:S(2)}) async-start(f32[32,16,128]{2,1,0:T(8,128)} %broadcast_in_dim.5), calls=%async_computation.3 | async-start | bytes 524288 | tf_op jit(solution)/shard_map/all_to_all | solution.py:295
  140.8 0.7 copy.15
  141.5 0.7 copy.14
  142.2 8.7 %all-to-all-done.3.rest_1_ = f32[32,16,128]{2,1,0:T(8,128)S(1)} async-done(((f32[32,16,128]{2,1,0:T(8,128)}), f32[32,16,128]{2,1,0:T(8,128)S(1)}, u32[]{:S(2)}, u32[]{:S(2)}) %all-to-all-start.3) | async-done | bytes 262176 | tf_op jit(solution)/shard_map/all_to_all | solution.py:295
  150.9 0.7 copy-done.2
  151.6 19.1 %respond.1 = bf16[8,4096,512]{2,1,0:T(8,128)(2,1)} custom-call(s32[12]{0:T(128)} %pad_add_fusion.places, f32[32,16,128]{2,1,0:T(8,128)} %copy-done.1, f32[32,16,128]{2,1,0:T(8,128)} %copy-done.2, f32[8,16,8]{2,1,0:T(8,128)} %bitcast.6, f32[8,16,8]{2,1,0:T(8,128)} %bitcast.5, bf16[4096,128]{1,0:T(8,128)(2,1)} %get-tuple-element.83.rest_4_, ...), custom_call_target="tpu_custom_call" | custom-call | flops 8589934592 | bytes 33554432 | tf_op jit(solution)/shard_map/respond/pallas_call | solution.py:255
  (126 shorter events, 4.5 us)
Async XLA Ops:
  0.0 140.3 %copy-start = (f32[64,8]{0,1:T(8,128)S(1)}, f32[64,8]{0,1:T(8,128)}, u32[]{:S(2)}) copy-start(f32[64,8]{0,1:T(8,128)} %param.16) | copy-start | bytes 6148
  6.5 5.2 %collective-permute-start = (bf16[256,256]{1,0:T(8,128)(2,1)}, bf16[256,256]{1,0:T(8,128)(2,1)S(1)}, u32[]{:S(2)}, u32[]{:S(2)}) collective-permute-start(bf16[256,256]{1,0:T(8,128)(2,1)} %get-tuple-element.46), channel_id=1, source_target_pairs={{0,1},{1,0},{2,3},{3,2},{4,5},{5,4},{6,7},{7,6},{8,9},{9,8},{10,11... | collective-permute-start | bytes 393224 | tf_op jit(solution)/shard_map/ppermute | solution.py:279
  7.0 7.1 %collective-permute-start.1 = (bf16[256,256]{1,0:T(8,128)(2,1)}, bf16[256,256]{1,0:T(8,128)(2,1)S(1)}, u32[]{:S(2)}, u32[]{:S(2)}) collective-permute-start(bf16[256,256]{1,0:T(8,128)(2,1)} %get-tuple-element.47), channel_id=1, source_target_pairs={{0,2},{1,3},{2,0},{3,1},{4,6},{5,7},{6,4},{7,5},{8,10},{9,11},{10,... | collective-permute-start | bytes 393224 | tf_op jit(solution)/shard_map/ppermute | solution.py:279
  9.5 6.9 %collective-permute-start.2 = (bf16[256,256]{1,0:T(8,128)(2,1)}, bf16[256,256]{1,0:T(8,128)(2,1)S(1)}, u32[]{:S(2)}, u32[]{:S(2)}) collective-permute-start(bf16[256,256]{1,0:T(8,128)(2,1)} %get-tuple-element.48), channel_id=1, source_target_pairs={{0,3},{1,2},{2,1},{3,0},{4,7},{5,6},{6,5},{7,4},{8,11},{9,10},{10,... | collective-permute-start | bytes 393224 | tf_op jit(solution)/shard_map/ppermute | solution.py:279
  9.6 14.0 %collective-permute-start.10 = (bf16[256,256]{1,0:T(8,128)(2,1)}, bf16[256,256]{1,0:T(8,128)(2,1)S(1)}, u32[]{:S(2)}, u32[]{:S(2)}) collective-permute-start(bf16[256,256]{1,0:T(8,128)(2,1)} %get-tuple-element.58), channel_id=1, source_target_pairs={{0,1},{1,0},{2,3},{3,2},{4,5},{5,4},{6,7},{7,6},{8,9},{9,8},{10,11... | collective-permute-start | bytes 393224 | tf_op jit(solution)/shard_map/ppermute | solution.py:279
  9.7 20.0 %collective-permute-start.11 = (bf16[256,256]{1,0:T(8,128)(2,1)}, bf16[256,256]{1,0:T(8,128)(2,1)S(1)}, u32[]{:S(2)}, u32[]{:S(2)}) collective-permute-start(bf16[256,256]{1,0:T(8,128)(2,1)} %get-tuple-element.59), channel_id=1, source_target_pairs={{0,2},{1,3},{2,0},{3,1},{4,6},{5,7},{6,4},{7,5},{8,10},{9,11},{10,... | collective-permute-start | bytes 393224 | tf_op jit(solution)/shard_map/ppermute | solution.py:279
  11.6 18.2 %collective-permute-start.12 = (bf16[256,256]{1,0:T(8,128)(2,1)}, bf16[256,256]{1,0:T(8,128)(2,1)S(1)}, u32[]{:S(2)}, u32[]{:S(2)}) collective-permute-start(bf16[256,256]{1,0:T(8,128)(2,1)} %get-tuple-element.60), channel_id=1, source_target_pairs={{0,3},{1,2},{2,1},{3,0},{4,7},{5,6},{6,5},{7,4},{8,11},{9,10},{10,... | collective-permute-start | bytes 393224 | tf_op jit(solution)/shard_map/ppermute | solution.py:279
  20.4 18.1 %copy-start.39 = (bf16[128,256]{1,0:T(8,128)(2,1)S(1)}, bf16[128,256]{1,0:T(8,128)(2,1)}, u32[]{:S(2)}) copy-start(bf16[128,256]{1,0:T(8,128)(2,1)} %get-tuple-element.55) | copy-start | bytes 196612
  20.4 23.0 %copy-start.38 = (bf16[128,256]{1,0:T(8,128)(2,1)S(1)}, bf16[128,256]{1,0:T(8,128)(2,1)}, u32[]{:S(2)}) copy-start(bf16[128,256]{1,0:T(8,128)(2,1)} %get-tuple-element.56) | copy-start | bytes 196612
  20.4 11.0 %collective-permute-start.3 = (bf16[128,256]{1,0:T(8,128)(2,1)}, bf16[128,256]{1,0:T(8,128)(2,1)S(1)}, u32[]{:S(2)}, u32[]{:S(2)}) collective-permute-start(bf16[128,256]{1,0:T(8,128)(2,1)} %get-tuple-element.50), channel_id=1, source_target_pairs={{0,4},{4,0},{8,12},{12,8},{16,20},{20,16},{24,28},{28,24},{1,5},{5... | collective-permute-start | bytes 196616 | tf_op jit(solution)/shard_map/ppermute | solution.py:279
  22.0 9.7 %collective-permute-start.4 = (bf16[128,256]{1,0:T(8,128)(2,1)}, bf16[128,256]{1,0:T(8,128)(2,1)S(1)}, u32[]{:S(2)}, u32[]{:S(2)}) collective-permute-start(bf16[128,256]{1,0:T(8,128)(2,1)} %get-tuple-element.51), channel_id=1, source_target_pairs={{0,8},{4,12},{8,0},{12,4},{16,24},{20,28},{24,16},{28,20},{1,9},{5... | collective-permute-start | bytes 196616 | tf_op jit(solution)/shard_map/ppermute | solution.py:279
  23.6 22.2 %copy-start.27 = (bf16[256,256]{1,0:T(8,128)(2,1)}, bf16[256,256]{1,0:T(8,128)(2,1)S(1)}, u32[]{:S(2)}) copy-start(bf16[256,256]{1,0:T(8,128)(2,1)S(1)} %collective-permute-done.10.rest_1_) | copy-start | bytes 393220
  23.6 10.9 %collective-permute-start.5 = (bf16[128,256]{1,0:T(8,128)(2,1)}, bf16[128,256]{1,0:T(8,128)(2,1)S(1)}, u32[]{:S(2)}, u32[]{:S(2)}) collective-permute-start(bf16[128,256]{1,0:T(8,128)(2,1)} %get-tuple-element.52), channel_id=1, source_target_pairs={{0,12},{4,8},{8,4},{12,0},{16,28},{20,24},{24,20},{28,16},{1,13},{... | collective-permute-start | bytes 196616 | tf_op jit(solution)/shard_map/ppermute | solution.py:279
  29.8 26.8 %collective-permute-start.20 = (bf16[256,512]{1,0:T(8,128)(2,1)}, bf16[256,512]{1,0:T(8,128)(2,1)S(1)}, u32[]{:S(2)}, u32[]{:S(2)}) collective-permute-start(bf16[256,512]{1,0:T(8,128)(2,1)} %get-tuple-element.71), channel_id=1, source_target_pairs={{0,1},{1,0},{2,3},{3,2},{4,5},{5,4},{6,7},{7,6},{8,9},{9,8},{10,11... | collective-permute-start | bytes 786440 | tf_op jit(solution)/shard_map/ppermute | solution.py:279
  29.9 29.1 %collective-permute-start.21 = (bf16[256,512]{1,0:T(8,128)(2,1)}, bf16[256,512]{1,0:T(8,128)(2,1)S(1)}, u32[]{:S(2)}, u32[]{:S(2)}) collective-permute-start(bf16[256,512]{1,0:T(8,128)(2,1)} %get-tuple-element.72), channel_id=1, source_target_pairs={{0,2},{1,3},{2,0},{3,1},{4,6},{5,7},{6,4},{7,5},{8,10},{9,11},{10,... | collective-permute-start | bytes 786440 | tf_op jit(solution)/shard_map/ppermute | solution.py:279
  31.4 37.2 %copy-start.10 = (bf16[128,256]{1,0:T(8,128)(2,1)}, bf16[128,256]{1,0:T(8,128)(2,1)S(1)}, u32[]{:S(2)}) copy-start(bf16[128,256]{1,0:T(8,128)(2,1)S(1)} %collective-permute-done.3.rest_1_) | copy-start | bytes 196612
  31.4 29.0 %collective-permute-start.22 = (bf16[256,512]{1,0:T(8,128)(2,1)}, bf16[256,512]{1,0:T(8,128)(2,1)S(1)}, u32[]{:S(2)}, u32[]{:S(2)}) collective-permute-start(bf16[256,512]{1,0:T(8,128)(2,1)} %get-tuple-element.73), channel_id=1, source_target_pairs={{0,3},{1,2},{2,1},{3,0},{4,7},{5,6},{6,5},{7,4},{8,11},{9,10},{10,... | collective-permute-start | bytes 786440 | tf_op jit(solution)/shard_map/ppermute | solution.py:279
  31.7 36.9 %copy-start.11 = (bf16[128,256]{1,0:T(8,128)(2,1)}, bf16[128,256]{1,0:T(8,128)(2,1)S(1)}, u32[]{:S(2)}) copy-start(bf16[128,256]{1,0:T(8,128)(2,1)S(1)} %collective-permute-done.4.rest_2_) | copy-start | bytes 196612
  31.7 6.7 %collective-permute-start.6 = (bf16[128,256]{1,0:T(8,128)(2,1)S(1)}, bf16[128,256]{1,0:T(8,128)(2,1)S(1)}, u32[]{:S(2)}, u32[]{:S(2)}) collective-permute-start(bf16[128,256]{1,0:T(8,128)(2,1)S(1)} %copy-done.41), channel_id=1, source_target_pairs={{0,16},{4,20},{8,24},{12,28},{16,0},{20,4},{24,8},{28,12},{1,17},{... | collective-permute-start | bytes 196616 | tf_op jit(solution)/shard_map/ppermute | solution.py:279
  34.4 34.2 %copy-start.12 = (bf16[128,256]{1,0:T(8,128)(2,1)}, bf16[128,256]{1,0:T(8,128)(2,1)S(1)}, u32[]{:S(2)}) copy-start(bf16[128,256]{1,0:T(8,128)(2,1)S(1)} %collective-permute-done.5.rest_3_) | copy-start | bytes 196612
  34.4 9.0 %collective-permute-start.7 = (bf16[128,256]{1,0:T(8,128)(2,1)S(1)}, bf16[128,256]{1,0:T(8,128)(2,1)S(1)}, u32[]{:S(2)}, u32[]{:S(2)}) collective-permute-start(bf16[128,256]{1,0:T(8,128)(2,1)S(1)} %copy-done.40), channel_id=1, source_target_pairs={{0,20},{4,16},{8,28},{12,24},{16,4},{20,0},{24,12},{28,8},{1,21},{... | collective-permute-start | bytes 196616 | tf_op jit(solution)/shard_map/ppermute | solution.py:279
  38.4 30.2 %copy-start.13 = (bf16[128,256]{1,0:T(8,128)(2,1)}, bf16[128,256]{1,0:T(8,128)(2,1)S(1)}, u32[]{:S(2)}) copy-start(bf16[128,256]{1,0:T(8,128)(2,1)S(1)} %collective-permute-done.6.rest_4_) | copy-start | bytes 196612
  38.5 10.5 %collective-permute-start.8 = (bf16[128,256]{1,0:T(8,128)(2,1)S(1)}, bf16[128,256]{1,0:T(8,128)(2,1)S(1)}, u32[]{:S(2)}, u32[]{:S(2)}) collective-permute-start(bf16[128,256]{1,0:T(8,128)(2,1)S(1)} %copy-done.39), channel_id=1, source_target_pairs={{0,24},{4,28},{8,16},{12,20},{16,8},{20,12},{24,0},{28,4},{1,25},{... | collective-permute-start | bytes 196616 | tf_op jit(solution)/shard_map/ppermute | solution.py:279
  43.4 25.2 %copy-start.14 = (bf16[128,256]{1,0:T(8,128)(2,1)}, bf16[128,256]{1,0:T(8,128)(2,1)S(1)}, u32[]{:S(2)}) copy-start(bf16[128,256]{1,0:T(8,128)(2,1)S(1)} %collective-permute-done.7.rest_5_) | copy-start | bytes 196612
  43.4 7.1 %collective-permute-start.9 = (bf16[128,256]{1,0:T(8,128)(2,1)S(1)}, bf16[128,256]{1,0:T(8,128)(2,1)S(1)}, u32[]{:S(2)}, u32[]{:S(2)}) collective-permute-start(bf16[128,256]{1,0:T(8,128)(2,1)S(1)} %copy-done.38), channel_id=1, source_target_pairs={{0,28},{4,24},{8,20},{12,16},{16,12},{20,8},{24,4},{28,0},{1,29},{... | collective-permute-start | bytes 196616 | tf_op jit(solution)/shard_map/ppermute | solution.py:279
  49.0 19.7 %copy-start.15 = (bf16[128,256]{1,0:T(8,128)(2,1)}, bf16[128,256]{1,0:T(8,128)(2,1)S(1)}, u32[]{:S(2)}) copy-start(bf16[128,256]{1,0:T(8,128)(2,1)S(1)} %collective-permute-done.8.rest_6_) | copy-start | bytes 196612
  49.0 4.5 %collective-permute-start.13 = (bf16[128,256]{1,0:T(8,128)(2,1)}, bf16[128,256]{1,0:T(8,128)(2,1)S(1)}, u32[]{:S(2)}, u32[]{:S(2)}) collective-permute-start(bf16[128,256]{1,0:T(8,128)(2,1)} %get-tuple-element.62), channel_id=1, source_target_pairs={{0,4},{4,0},{8,12},{12,8},{16,20},{20,16},{24,28},{28,24},{1,5},{5... | collective-permute-start | bytes 196616 | tf_op jit(solution)/shard_map/ppermute | solution.py:279
  50.6 18.1 %copy-start.16 = (bf16[128,256]{1,0:T(8,128)(2,1)}, bf16[128,256]{1,0:T(8,128)(2,1)S(1)}, u32[]{:S(2)}) copy-start(bf16[128,256]{1,0:T(8,128)(2,1)S(1)} %collective-permute-done.9.rest_7_) | copy-start | bytes 196612
  50.6 4.5 %collective-permute-start.14 = (bf16[128,256]{1,0:T(8,128)(2,1)}, bf16[128,256]{1,0:T(8,128)(2,1)S(1)}, u32[]{:S(2)}, u32[]{:S(2)}) collective-permute-start(bf16[128,256]{1,0:T(8,128)(2,1)} %get-tuple-element.63), channel_id=1, source_target_pairs={{0,8},{4,12},{8,0},{12,4},{16,24},{20,28},{24,16},{28,20},{1,9},{5... | collective-permute-start | bytes 196616 | tf_op jit(solution)/shard_map/ppermute | solution.py:279
  53.5 13.4 %collective-permute-start.15 = (bf16[128,256]{1,0:T(8,128)(2,1)}, bf16[128,256]{1,0:T(8,128)(2,1)S(1)}, u32[]{:S(2)}, u32[]{:S(2)}) collective-permute-start(bf16[128,256]{1,0:T(8,128)(2,1)} %get-tuple-element.64), channel_id=1, source_target_pairs={{0,12},{4,8},{8,4},{12,0},{16,28},{20,24},{24,20},{28,16},{1,13},{... | collective-permute-start | bytes 196616 | tf_op jit(solution)/shard_map/ppermute | solution.py:279
  55.0 13.5 %collective-permute-start.16 = (bf16[128,256]{1,0:T(8,128)(2,1)}, bf16[128,256]{1,0:T(8,128)(2,1)S(1)}, u32[]{:S(2)}, u32[]{:S(2)}) collective-permute-start(bf16[128,256]{1,0:T(8,128)(2,1)} %get-tuple-element.65), channel_id=1, source_target_pairs={{0,16},{4,20},{8,24},{12,28},{16,0},{20,4},{24,8},{28,12},{1,17},{... | collective-permute-start | bytes 196616 | tf_op jit(solution)/shard_map/ppermute | solution.py:279
  56.6 11.9 %collective-permute-start.17 = (bf16[128,256]{1,0:T(8,128)(2,1)}, bf16[128,256]{1,0:T(8,128)(2,1)S(1)}, u32[]{:S(2)}, u32[]{:S(2)}) collective-permute-start(bf16[128,256]{1,0:T(8,128)(2,1)} %get-tuple-element.66), channel_id=1, source_target_pairs={{0,20},{4,16},{8,28},{12,24},{16,4},{20,0},{24,12},{28,8},{1,21},{... | collective-permute-start | bytes 196616 | tf_op jit(solution)/shard_map/ppermute | solution.py:279
  58.9 9.6 %collective-permute-start.18 = (bf16[128,256]{1,0:T(8,128)(2,1)}, bf16[128,256]{1,0:T(8,128)(2,1)S(1)}, u32[]{:S(2)}, u32[]{:S(2)}) collective-permute-start(bf16[128,256]{1,0:T(8,128)(2,1)} %get-tuple-element.67), channel_id=1, source_target_pairs={{0,24},{4,28},{8,16},{12,20},{16,8},{20,12},{24,0},{28,4},{1,25},{... | collective-permute-start | bytes 196616 | tf_op jit(solution)/shard_map/ppermute | solution.py:279
  60.5 8.1 %collective-permute-start.19 = (bf16[128,256]{1,0:T(8,128)(2,1)}, bf16[128,256]{1,0:T(8,128)(2,1)S(1)}, u32[]{:S(2)}, u32[]{:S(2)}) collective-permute-start(bf16[128,256]{1,0:T(8,128)(2,1)} %get-tuple-element.68), channel_id=1, source_target_pairs={{0,28},{4,24},{8,20},{12,16},{16,12},{20,8},{24,4},{28,0},{1,29},{... | collective-permute-start | bytes 196616 | tf_op jit(solution)/shard_map/ppermute | solution.py:279
  66.9 18.8 %copy-start.30 = (bf16[128,512]{1,0:T(8,128)(2,1)S(1)}, bf16[128,512]{1,0:T(8,128)(2,1)}, u32[]{:S(2)}) copy-start(bf16[128,512]{1,0:T(8,128)(2,1)} %get-tuple-element.81) | copy-start | bytes 393220
  66.9 16.4 %collective-permute-start.23 = (bf16[128,512]{1,0:T(8,128)(2,1)}, bf16[128,512]{1,0:T(8,128)(2,1)S(1)}, u32[]{:S(2)}, u32[]{:S(2)}) collective-permute-start(bf16[128,512]{1,0:T(8,128)(2,1)} %get-tuple-element.75), channel_id=1, source_target_pairs={{0,4},{4,0},{8,12},{12,8},{16,20},{20,16},{24,28},{28,24},{1,5},{5... | collective-permute-start | bytes 393224 | tf_op jit(solution)/shard_map/ppermute | solution.py:279
  68.5 17.2 %collective-permute-start.24 = (bf16[128,512]{1,0:T(8,128)(2,1)}, bf16[128,512]{1,0:T(8,128)(2,1)S(1)}, u32[]{:S(2)}, u32[]{:S(2)}) collective-permute-start(bf16[128,512]{1,0:T(8,128)(2,1)} %get-tuple-element.76), channel_id=1, source_target_pairs={{0,8},{4,12},{8,0},{12,4},{16,24},{20,28},{24,16},{28,20},{1,9},{5... | collective-permute-start | bytes 393224 | tf_op jit(solution)/shard_map/ppermute | solution.py:279
  73.5 66.9 %copy-start.42 = (s32[256]{0:T(256)S(1)}, s32[256]{0:T(256)}, u32[]{:S(2)}) copy-start(s32[256]{0:T(256)} %param.15) | copy-start | bytes 3076
  73.5 33.8 %all-to-all-start = ((bf16[32,16,128]{2,1,0:T(8,128)(2,1)}), bf16[32,16,128]{2,1,0:T(8,128)(2,1)S(1)}, u32[]{:S(2)}, u32[]{:S(2)}) async-start(bf16[32,16,128]{2,1,0:T(8,128)(2,1)} %get-tuple-element.69), calls=%async_computation | async-start | bytes 262144 | tf_op jit(solution)/shard_map/all_to_all | solution.py:292
  77.6 11.9 %collective-permute-start.25 = (bf16[128,512]{1,0:T(8,128)(2,1)S(1)}, bf16[128,512]{1,0:T(8,128)(2,1)S(1)}, u32[]{:S(2)}, u32[]{:S(2)}) collective-permute-start(bf16[128,512]{1,0:T(8,128)(2,1)S(1)} %copy-done.34), channel_id=1, source_target_pairs={{0,12},{4,8},{8,4},{12,0},{16,28},{20,24},{24,20},{28,16},{1,13},{... | collective-permute-start | bytes 393224 | tf_op jit(solution)/shard_map/ppermute | solution.py:279
  80.3 18.6 %collective-permute-start.26 = (bf16[128,512]{1,0:T(8,128)(2,1)S(1)}, bf16[128,512]{1,0:T(8,128)(2,1)S(1)}, u32[]{:S(2)}, u32[]{:S(2)}) collective-permute-start(bf16[128,512]{1,0:T(8,128)(2,1)S(1)} %copy-done.33), channel_id=1, source_target_pairs={{0,16},{4,20},{8,24},{12,28},{16,0},{20,4},{24,8},{28,12},{1,17},{... | collective-permute-start | bytes 393224 | tf_op jit(solution)/shard_map/ppermute | solution.py:279
  82.8 19.4 %collective-permute-start.27 = (bf16[128,512]{1,0:T(8,128)(2,1)S(1)}, bf16[128,512]{1,0:T(8,128)(2,1)S(1)}, u32[]{:S(2)}, u32[]{:S(2)}) collective-permute-start(bf16[128,512]{1,0:T(8,128)(2,1)S(1)} %copy-done.32), channel_id=1, source_target_pairs={{0,20},{4,16},{8,28},{12,24},{16,4},{20,0},{24,12},{28,8},{1,21},{... | collective-permute-start | bytes 393224 | tf_op jit(solution)/shard_map/ppermute | solution.py:279
  83.3 19.0 %copy-start.3 = (bf16[128,512]{1,0:T(8,128)(2,1)}, bf16[128,512]{1,0:T(8,128)(2,1)S(1)}, u32[]{:S(2)}) copy-start(bf16[128,512]{1,0:T(8,128)(2,1)S(1)} %collective-permute-done.23.rest_1_) | copy-start | bytes 393220
  83.3 19.0 %collective-permute-start.28 = (bf16[128,512]{1,0:T(8,128)(2,1)S(1)}, bf16[128,512]{1,0:T(8,128)(2,1)S(1)}, u32[]{:S(2)}, u32[]{:S(2)}) collective-permute-start(bf16[128,512]{1,0:T(8,128)(2,1)S(1)} %copy-done.31), channel_id=1, source_target_pairs={{0,24},{4,28},{8,16},{12,20},{16,8},{20,12},{24,0},{28,4},{1,25},{... | collective-permute-start | bytes 393224 | tf_op jit(solution)/shard_map/ppermute | solution.py:279
  85.7 16.5 %collective-permute-start.29 = (bf16[128,512]{1,0:T(8,128)(2,1)S(1)}, bf16[128,512]{1,0:T(8,128)(2,1)S(1)}, u32[]{:S(2)}, u32[]{:S(2)}) collective-permute-start(bf16[128,512]{1,0:T(8,128)(2,1)S(1)} %copy-done.30), channel_id=1, source_target_pairs={{0,28},{4,24},{8,20},{12,16},{16,12},{20,8},{24,4},{28,0},{1,29},{... | collective-permute-start | bytes 393224 | tf_op jit(solution)/shard_map/ppermute | solution.py:279
  107.3 15.8 %all-to-all-start.2 = ((bf16[32,16,128]{2,1,0:T(8,128)(2,1)}), bf16[32,16,128]{2,1,0:T(8,128)(2,1)S(1)}, u32[]{:S(2)}, u32[]{:S(2)}) async-start(bf16[32,16,128]{2,1,0:T(8,128)(2,1)} %get-tuple-element.82), calls=%async_computation.2 | async-start | bytes 262144 | tf_op jit(solution)/shard_map/all_to_all | solution.py:292
  123.8 13.2 %all-to-all-start.1 = ((f32[32,16,128]{2,1,0:T(8,128)}), f32[32,16,128]{2,1,0:T(8,128)S(1)}, u32[]{:S(2)}, u32[]{:S(2)}) async-start(f32[32,16,128]{2,1,0:T(8,128)} %broadcast_in_dim.4), calls=%async_computation.1 | async-start | bytes 524288 | tf_op jit(solution)/shard_map/all_to_all | solution.py:295
  137.7 13.2 %all-to-all-start.3 = ((f32[32,16,128]{2,1,0:T(8,128)}), f32[32,16,128]{2,1,0:T(8,128)S(1)}, u32[]{:S(2)}, u32[]{:S(2)}) async-start(f32[32,16,128]{2,1,0:T(8,128)} %broadcast_in_dim.5), calls=%async_computation.3 | async-start | bytes 524288 | tf_op jit(solution)/shard_map/all_to_all | solution.py:295
  (29 other events, 216.3 us)
where the time goes:
time: 172 us; the launch traced here: 171 us
  starting transfers between devices  60.1 us (35%)
  waiting for transfers between devices  53.5 us (31%)
  Pallas kernels  49.9 us (29%)
  local copies, waits for them, and re-layouts  5.82 us (3%)
    ppermute x30, starting transfers between devices, exchange(): lax.ppermute(blocks[s], axis, [(i, i ^ s) for i in range(size)])  43.2 us
    ppermute x30, waiting for transfers between devices, exchange(): lax.ppermute(blocks[s], axis, [(i, i ^ s) for i in range(size)])  26.1 us
    all_to_all x2, waiting for transfers between devices, sum_shares(): return lax.all_to_all(spread, both, 0, 0, tiled=True)  19.2 us
    pallas_call x1, Pallas kernels, respond(): pl.pallas_call(functools.partial(respond_kernel, blocks, slabs, groups, f...  19.1 us
    all_to_all x2, starting transfers between devices, sum_shares(): taken = lax.all_to_all(shares, both, 0, 0, tiled=True)  11.7 us
    pallas_call x2, Pallas kernels, front(): pl.pallas_call(functools.partial(front_kernel, start, slabs, widths), out...  11.6 us
    pallas_call x3, Pallas kernels, across(): pl.pallas_call(functools.partial(across_kernel, slabs, blocks, first, gri...  10.7 us
    pallas_call x2, Pallas kernels, project(): pl.pallas_call(functools.partial(project_kernel, blocks, slabs, widths),...  8.55 us
  transfers between devices with their start and end apart: 34, of which 11 were waited for; matrix products, arithmetic and copies ran while one was open for 1% of the time, Pallas kernels for 15%

commit v1 on v0

v1 whole, which is shorter than its diff:
```python
import functools
import math

import jax
import jax.numpy as jnp
import numpy as np
from jax import lax
from jax.experimental import pallas as pl
from jax.experimental.pallas import tpu as pltpu
from jax.sharding import PartitionSpec as P

GROUP = 16
LANES = 128
SPLITS = ((1,), (1,))
WHOLE = ((False,), (False,))
PERMUTE_MOST = 8
MIB = 1024 * 1024
COST = pl.CostEstimate(flops=1, bytes_accessed=1, transcendentals=0)
F32 = jnp.float32
BF16 = jnp.bfloat16


def rounded(values):
    return np.asarray(values, np.float32).astype(jnp.bfloat16)


def tables(grid, slabs):
    scaling = np.float32(1.0 / math.sqrt(grid))
    step = np.float32(2.0 * math.pi / grid)
    at = np.arange(grid)
    half = np.arange(grid // 2)

    def cos_sin(a, b):
        angle = (a[:, None] * b[None, :] % grid).astype(np.float32) * step
        return (
            rounded(np.cos(angle) * scaling).astype(np.float32),
            rounded(np.sin(angle) * scaling).astype(np.float32),
        )

    planes = grid // slabs
    depth = grid // 2 // slabs
    channels = 2 * depth
    group = LANES // channels
    zc, zs = cos_sin(at, half)
    ztab = np.stack([zc, -zs], -1).reshape(grid, slabs, channels)
    zmat = np.einsum("ab,znq->aznbq", np.eye(group, dtype=np.float32), ztab)
    zmat = zmat.reshape(group * grid, slabs * group * channels)
    signed = np.where(half < grid // 4, half, half - grid // 2)
    yc, ys = cos_sin(signed, at)
    mix = np.zeros((grid, 2, grid // 2, 2), np.float32)
    mix[:, 0, :, 0] = yc.T
    mix[:, 1, :, 0] = ys.T
    mix[:, 0, :, 1] = -ys.T
    mix[:, 1, :, 1] = yc.T
    ymat = np.einsum("yajb,dk->ydajkb", mix, np.eye(depth, dtype=np.float32))
    ymat = ymat.reshape(grid * channels, grid // 2 * channels)
    xc, xs = cos_sin(at, at)
    xtab = np.stack([xc, xs]).reshape(2, grid, slabs, planes)
    xmat = np.einsum("hksx,pr->skphrx", xtab, np.eye(8, dtype=np.float32))
    xmat = xmat.reshape(slabs, grid * 8, 2 * 8 * planes)
    swap = np.zeros((2 * LANES, 2 * LANES), np.float32)
    even = np.arange(0, 2 * LANES, 2)
    swap[even + 1, even] = 1.0
    swap[even, even + 1] = -1.0
    return rounded(zmat), rounded(ymat), rounded(xmat), rounded(swap)


def partners(slabs, blocks):
    narrow, wide = lax.axis_index("narrow"), lax.axis_index("wide")
    return [narrow ^ s for s in range(slabs)] + [wide ^ s for s in range(blocks)]


def views(refs, places, first, count):
    found = []
    for ref in refs:
        if len(ref.shape) == 3:
            found += [ref.at[places[first + s]] for s in range(count)]
        else:
            found.append(ref)
    return found


def shapes(count, height, wide, whole):
    if whole or count > PERMUTE_MOST:
        return [jax.ShapeDtypeStruct((count, height, wide), BF16)]
    return [jax.ShapeDtypeStruct((height, wide), BF16)] * count


def front_kernel(start, slabs, widths, occ_at, emp_at, *rest):
    count = len(rest) - 11
    outs, (prod, lines) = rest[4 : 4 + count], rest[4 + count : 6 + count]
    held, arrived = rest[6 + count : 10 + count], rest[10 + count]
    occ, emp, zmat, ymat = held
    planes = occ.shape[1]
    width = zmat.shape[0]
    steps = occ.shape[2] // width
    mats = [pltpu.make_async_copy(rest[2 + i], held[2 + i], arrived.at[i]) for i in range(2)]
    pieces = []
    for g in range(steps):
        lanes = slice(g * width, (g + 1) * width)
        pieces.append(
            [
                pltpu.make_async_copy(
                    rest[i].at[:, :, lanes], held[i].at[:, :, lanes], arrived.at[2 + 2 * g + i]
                )
                for i in range(2)
            ]
        )
    pieces[0][0].start()
    pieces[0][1].start()
    mats[0].start()
    for piece in pieces[1:]:
        piece[0].start()
        piece[1].start()
    mats[1].start()
    places = partners(slabs, 1)
    outs = views(outs, places, 0, slabs)
    for g in range(steps):
        lanes = slice(g * width, (g + 1) * width)
        pieces[g][0].wait()
        pieces[g][1].wait()
        for p in range(GROUP):
            o, e = occ_at[start + p], emp_at[start + p]
            prod[p * planes : (p + 1) * planes, :] = (
                occ[o, :, lanes].astype(F32) * emp[e, :, lanes].astype(F32)
            ).astype(BF16)
        if g == 0:
            mats[0].wait()
        along = jnp.dot(prod[...], zmat[...], preferred_element_type=F32).astype(BF16)
        for n in range(slabs):
            lines[n, :, g * LANES : (g + 1) * LANES] = along[:, n * LANES : (n + 1) * LANES]
    mats[1].wait()
    for s in range(slabs):
        along = jnp.dot(lines[places[s]], ymat[...], preferred_element_type=F32).astype(BF16)
        first = 0
        for h, wide in enumerate(widths):
            outs[h * slabs + s][...] = along[:, first : first + wide]
            first += wide


def front(start, slabs, widths, occ_at, emp_at, *held):
    occ, _, zmat, ymat = held
    rows = GROUP * occ.shape[1]
    width = zmat.shape[0]
    steps = occ.shape[2] // width
    smem = pl.BlockSpec(memory_space=pltpu.SMEM)
    vmem = pl.BlockSpec(memory_space=pltpu.VMEM)
    out_shape = [o for w in widths for o in shapes(slabs, rows, w, False)]
    outs = pl.pallas_call(
        functools.partial(front_kernel, start, slabs, widths),
        out_shape=out_shape,
        in_specs=[smem] * 2 + [pl.BlockSpec(memory_space=pl.ANY)] * 4,
        out_specs=[vmem] * len(out_shape),
        scratch_shapes=[
            pltpu.VMEM((rows, width), BF16),
            pltpu.VMEM((slabs, rows, ymat.shape[0]), BF16),
        ]
        + [pltpu.VMEM(h.shape, BF16) for h in held]
        + [pltpu.SemaphoreType.DMA((2 + 2 * steps,))],
        compiler_params=pltpu.CompilerParams(vmem_limit_bytes=56 * MIB),
        cost_estimate=COST,
        name="front",
    )(occ_at, emp_at, *held)
    each = len(outs) // len(widths)
    return [outs[h * each : (h + 1) * each] for h in range(len(widths))]


def across_kernel(slabs, blocks, first, grid, taken, after, *rest):
    places = partners(slabs, blocks)
    parts = views(rest[:taken], places, 0, slabs)
    xmat, swap = rest[taken : taken + 2]
    outs, whole = views(rest[taken + 2 + after : -1], places, slabs, blocks), rest[-1]
    rows, wide = parts[0].shape
    planes = rows // GROUP
    half = grid // 2
    channels = 2 * (half // slabs)
    lane = first + lax.broadcasted_iota(jnp.int32, (grid, wide), 1)
    kx = lax.broadcasted_iota(jnp.int32, (grid, wide), 0)
    kx = jnp.where(kx < half, kx, kx - grid)
    ky = lane // channels
    ky = jnp.where(ky < half // 2, ky, ky - half)
    kz = places[0] * (channels // 2) + lane % channels // 2
    squared = (kx * kx + ky * ky + kz * kz).astype(F32)
    quarter = float(grid // 4)
    coulomb = (1.0 / jnp.sqrt(1.0 + squared / (quarter * quarter)))[:, None, :]
    left = jnp.concatenate([xmat[places[s]] for s in range(slabs)], axis=1)
    found = []
    for m in range(GROUP // 8):
        right = []
        for s in range(slabs):
            plain = parts[s][m * 8 * planes : (m + 1) * 8 * planes, :]
            right.append(plain)
            turned = [
                jnp.dot(plain[:, c : c + 2 * LANES], swap[...], preferred_element_type=F32)
                for c in range(0, wide, 2 * LANES)
            ]
            right.append(jnp.concatenate(turned, axis=1).astype(BF16))
        right = jnp.concatenate(right, axis=0)
        total = jnp.dot(left, right, preferred_element_type=F32)
        found.append(total.reshape(grid, 8, wide) * coulomb)
    found = jnp.concatenate(found, axis=1).astype(BF16)
    whole[...] = found.reshape(whole.shape)
    for s in range(blocks):
        outs[s][...] = whole[places[slabs + s]]


def across(slabs, blocks, first, grid, parts, xmat, swap, whole, after):
    rows, wide = parts[0].shape[-2:]
    tall = grid // blocks * GROUP
    out_shape = shapes(blocks, tall, wide, whole)
    vmem = pl.BlockSpec(memory_space=pltpu.VMEM)
    return pl.pallas_call(
        functools.partial(across_kernel, slabs, blocks, first, grid, len(parts), len(after)),
        out_shape=out_shape,
        in_specs=[vmem] * (len(parts) + 2)
        + [pl.BlockSpec(memory_space=pl.ANY)] * len(after),
        out_specs=[vmem] * len(out_shape),
        scratch_shapes=[pltpu.VMEM((blocks, tall, wide), BF16)],
        compiler_params=pltpu.CompilerParams(vmem_limit_bytes=24 * MIB),
        cost_estimate=COST,
        name="across",
    )(*parts, xmat, swap, *after)


def project_kernel(blocks, slabs, widths, after, held, trial, *rest):
    shares = rest[-1]
    parts, earlier = rest[: -1 - after - held], rest[-1 - after - held : -1 - after]
    places = partners(slabs, blocks)
    parts = views(parts, places, slabs, blocks)
    for ref in earlier:
        shares[:, : ref.shape[1], :] = ref[...]
    below = shares.shape[1] - GROUP
    lanes = sum(widths)
    heights = parts[0].shape[0] // GROUP
    total = jnp.zeros((blocks * GROUP, trial.shape[1]), F32)
    for x in range(heights):
        first = x * lanes
        for h, wide in enumerate(widths):
            left = jnp.concatenate(
                [parts[h * blocks + s][x * GROUP : (x + 1) * GROUP, :] for s in range(blocks)], axis=0
            )
            total += jnp.dot(left, trial[first : first + wide, :], preferred_element_type=F32)
            first += wide
    step = trial.shape[1] // slabs
    for s in range(blocks):
        for n in range(slabs):
            shares[places[slabs + s] * slabs + n, below:, :] = total[
                s * GROUP : (s + 1) * GROUP, n * step : (n + 1) * step
            ].astype(shares.dtype)


def project(blocks, slabs, widths, trial, parts, earlier, after):
    columns, vectors = trial.shape
    pairs = blocks * GROUP
    height = GROUP + sum(e.shape[1] for e in earlier)
    vmem = pl.BlockSpec(memory_space=pltpu.VMEM)
    return pl.pallas_call(
        functools.partial(project_kernel, blocks, slabs, widths, len(after), len(earlier)),
        out_shape=jax.ShapeDtypeStruct((blocks * slabs, height, vectors // slabs), BF16),
        in_specs=[vmem] * (1 + len(parts) + len(earlier))
        + [pl.BlockSpec(memory_space=pl.ANY)] * len(after),
        out_specs=vmem,
        compiler_params=pltpu.CompilerParams(vmem_limit_bytes=24 * MIB),
        cost_estimate=COST,
        name="project",
    )(trial, *parts, *earlier, *after)


def turn_kernel(blocks, slabs, widths, *rest):
    places = partners(slabs, blocks)
    parts, turned = views(rest[:-1], places, slabs, blocks), rest[-1]
    lanes = sum(widths)
    for x in range(parts[0].shape[0] // GROUP):
        first = x * lanes
        for h, wide in enumerate(widths):
            left = [parts[h * blocks + s][x * GROUP : (x + 1) * GROUP, :] for s in range(blocks)]
            turned[first : first + wide, :] = jnp.concatenate(left, axis=0).T
            first += wide


def turn(blocks, slabs, widths, columns, parts):
    vmem = pl.BlockSpec(memory_space=pltpu.VMEM)
    return pl.pallas_call(
        functools.partial(turn_kernel, blocks, slabs, widths),
        out_shape=jax.ShapeDtypeStruct((columns, blocks * GROUP), BF16),
        in_specs=[vmem] * len(parts),
        out_specs=vmem,
        compiler_params=pltpu.CompilerParams(vmem_limit_bytes=16 * MIB),
        cost_estimate=COST,
        name="turn",
    )(*parts)


def respond_kernel(blocks, slabs, groups, freqs, *rest):
    shares, weights, turned = rest[0], rest[1], rest[2 : groups + 2]
    out, weighted = rest[groups + 2 :]
    places = partners(slabs, blocks)
    vectors = out.shape[2]
    step = vectors // slabs

    @pl.when(pl.program_id(0) == 0)
    def _():
        for g in range(groups):
            for s in range(blocks):
                source = places[slabs + s]
                row = (g * blocks + s) * GROUP
                scale = weights[source, g]
                for n in range(slabs):
                    share = shares[source * slabs + n, g * GROUP : (g + 1) * GROUP, :].astype(F32)
                    for w in range(freqs):
                        weighted[w, row : row + GROUP, n * step : (n + 1) * step] = (
                            scale[:, w : w + 1] * share
                        ).astype(BF16)

    left = jnp.concatenate([t[...] for t in turned], axis=1)
    for w in range(freqs):
        out[w] = jnp.dot(left, weighted[w], preferred_element_type=F32).astype(BF16)


def respond(blocks, slabs, shares, weights, turned, vectors):
    groups = len(turned)
    columns, pairs = turned[0].shape
    freqs = weights.shape[-1]
    height = min(columns, 512)
    vmem = pl.BlockSpec(memory_space=pltpu.VMEM)
    return pl.pallas_call(
        functools.partial(respond_kernel, blocks, slabs, groups, freqs),
        grid=(columns // height,),
        out_shape=jax.ShapeDtypeStruct((freqs, columns, vectors), BF16),
        in_specs=[vmem] * 2
        + [pl.BlockSpec((height, pairs), lambda i: (i, 0))] * groups,
        out_specs=pl.BlockSpec((freqs, height, vectors), lambda i: (0, i, 0)),
        scratch_shapes=[pltpu.VMEM((freqs, groups * pairs, vectors), BF16)],
        compiler_params=pltpu.CompilerParams(vmem_limit_bytes=16 * MIB + 4 * freqs * vectors * (groups * pairs + height)),
        cost_estimate=COST,
        name="respond",
    )(shares, weights, *turned)


def exchange(blocks, axis):
    if len(blocks) == 1:
        return [lax.all_to_all(blocks[0], axis, 0, 0, tiled=True)]
    return [blocks[0]] + [
        lax.ppermute(blocks[s], axis, [(i, i ^ s) for i in range(len(blocks))])
        for s in range(1, len(blocks))
    ]


def sum_shares(shares):
    both = ("wide", "narrow")
    count = shares.shape[0]
    taken = lax.all_to_all(shares, both, 0, 0, tiled=True)
    total = jnp.sum(taken.astype(F32), axis=0, keepdims=True).astype(BF16)
    spread = jnp.broadcast_to(total, (count,) + total.shape[1:])
    return lax.all_to_all(spread, both, 0, 0, tiled=True)


def shards(occupied, empty, pair_occ, pair_emp, pair_level, denominators, trial):
    slabs = lax.axis_size("narrow")
    blocks = lax.axis_size("wide")
    grid = occupied.shape[1] * slabs
    zmat, ymat, xmat, swap = (jnp.asarray(t) for t in tables(grid, slabs))
    lanes = ymat.shape[1]
    groups = pair_occ.shape[0] // GROUP
    vectors = trial.shape[1]
    levels = jnp.arange(denominators.shape[0], dtype=jnp.int32)
    onehot = (pair_level[:, None] == levels[None, :]).astype(F32)
    weights = jnp.dot(onehot, denominators, precision=lax.Precision.HIGHEST)
    weights = weights.reshape(blocks, groups, GROUP, -1)

    sent, waves = {}, {}
    for g in range(groups):
        cut = SPLITS[g % len(SPLITS)]
        widths = tuple(lanes * c // sum(cut) for c in cut)
        sent[g] = widths, front(
            g * GROUP, slabs, widths, pair_occ, pair_emp, occupied, empty, zmat, ymat
        )
    for g in range(groups):
        first, waves[g] = 0, []
        after = [blocked[0] for blocked in sent[g + 1][1]] if g + 1 < groups else []
        for whole, wide, blocked in zip(WHOLE[g % len(WHOLE)], *sent[g]):
            got = exchange(blocked, "narrow")
            waves[g].append(
                across(slabs, blocks, first, grid, got, xmat, swap, whole, after)
            )
            first += wide
    shares, turned = [], []
    for g in range(groups):
        parts = [piece for blocked in waves[g] for piece in exchange(blocked, "wide")]
        after = [blocked[0] for blocked in waves.get(g + 1, [])]
        widths = sent[g][0]
        shares = [project(blocks, slabs, widths, trial, parts, shares, after)]
        turned.append(turn(blocks, slabs, widths, trial.shape[0], parts))
    shares = sum_shares(shares[0])
    return respond(
        blocks,
        slabs,
        shares,
        weights,
        turned,
        vectors,
    )


def solution(mesh):
    placed = (
        P("wide", "narrow", None),
        P("wide", "narrow", None),
        P("wide"),
        P("wide"),
        P(),
        P(),
        P(("wide", "narrow"), None),
    )
    return jax.shard_map(
        shards,
        mesh=mesh,
        in_specs=placed,
        out_specs=P(None, ("wide", "narrow"), None),
        check_vma=False,
    )
```

time: 172 us -> 125 us (0.73)
  starting transfers between devices: 60.1 us -> 36.8 us
  waiting for transfers between devices: 53.5 us -> 31.7 us
  blocking collectives: 0 us -> 19.5 us
  Pallas kernels: 49.9 us -> 34.2 us
  local copies, waits for them, and re-layouts: 5.82 us -> 1.71 us
    all_to_all x0 -> x1, blocking collectives: none -> 19.5 us  [sum_shares(): taken = lax.all_to_all(shares, both, 0, 0, tiled=True)]
    all_to_all x2 -> x0, starting transfers between devices: 11.7 us -> none  [sum_shares(): taken = lax.all_to_all(shares, both, 0, 0, tiled=True)]
    all_to_all x2 -> x1, waiting for transfers between devices: 19.2 us -> 9.66 us  [sum_shares(): return lax.all_to_all(spread, both, 0, 0, tiled=True)]
    ppermute x30 -> x20, starting transfers between devices: 43.2 us -> 34.2 us  [exchange(): lax.ppermute(blocks[s], axis, [(i, i ^ s) for i in range(len(blocks))])]
    all_to_all x2 -> x0, waiting for transfers between devices: 8.19 us -> none  [sum_shares(): taken = lax.all_to_all(shares, both, 0, 0, tiled=True)]
    pallas_call x3 -> x2, Pallas kernels: 10.7 us -> 3.31 us  [across(): pl.pallas_call(functools.partial(across_kernel, slabs, blocks, first, gri...]
    pallas_call x2 -> x4, Pallas kernels: 8.55 us -> 2.08 us  [the longest x2 1.43 us: project(): pl.pallas_call(functools.partial(project_kernel, blocks, slabs, widths, l...]
    pallas_call x1, Pallas kernels: 19.1 us -> 15 us  [respond(): pl.pallas_call(functools.partial(respond_kernel, blocks, slabs, groups, f...]
  transfers between devices with their start and end apart: 34 -> 21, of which waited for: 11 -> 5; matrix products, arithmetic and copies ran while one was open for 1% -> 0% of each run, Pallas kernels for 15% -> 9%
where the time goes in v1:
time: 125 us; the launch traced here: 124 us
  starting transfers between devices  36.8 us (29%)
  Pallas kernels  34.2 us (27%)
  waiting for transfers between devices  31.7 us (25%)
  blocking collectives  19.5 us (16%)
  local copies, waits for them, and re-layouts  1.71 us (1%)
    ppermute x20, starting transfers between devices, exchange(): lax.ppermute(blocks[s], axis, [(i, i ^ s) for i in range(len(blocks))])  34.2 us
    ppermute x20, waiting for transfers between devices, exchange(): lax.ppermute(blocks[s], axis, [(i, i ^ s) for i in range(len(blocks))])  22 us
    all_to_all x1, blocking collectives, sum_shares(): taken = lax.all_to_all(shares, both, 0, 0, tiled=True)  19.5 us
    pallas_call x1, Pallas kernels, respond(): pl.pallas_call(functools.partial(respond_kernel, blocks, slabs, groups, f...  15 us
    pallas_call x2, Pallas kernels, front(): pl.pallas_call(functools.partial(front_kernel, start, slabs, widths), out...  13.8 us
    all_to_all x1, waiting for transfers between devices, sum_shares(): return lax.all_to_all(spread, both, 0, 0, tiled=True)  9.66 us
    pallas_call x2, Pallas kernels, across(): pl.pallas_call(functools.partial(across_kernel, slabs, blocks, first, gri...  3.31 us
    all_to_all x1, starting transfers between devices, sum_shares(): return lax.all_to_all(spread, both, 0, 0, tiled=True)  2.59 us
  transfers between devices with their start and end apart: 21, of which 5 were waited for; matrix products, arithmetic and copies ran while one was open for 0% of the time, Pallas kernels for 9%

profile of v1, /device:TPU:0, one launch (start us, length us, event | category | flops | bytes accessed | tf_op | source)
XLA Modules:
  0.0 124.3 jit_solution(13663170885620942653)
XLA Ops:
  0.0 6.7 %front.3 = (bf16[256,512]{1,0:T(8,128)(2,1)}, bf16[256,512]{1,0:T(8,128)(2,1)}, bf16[256,512]{1,0:T(8,128)(2,1)}, bf16[256,512]{1,0:T(8,128)(2,1)}) custom-call(s32[32]{0:T(128)} %occ_at.3, s32[32]{0:T(128)} %emp_at.3, bf16[8,16,4096]{2,1,0:T(8,128)(2,1)} %rest_0_.3, bf16[16,16,4096]{2,1,0:T(8,128)(2,1)} %rest_1_.3, ...), custom_call_target="tpu_custom_call" | custom-call | flops 1 | bytes 1 | tf_op jit(solution)/shard_map/front/pallas_call | solution.py:149
  6.7 0.5 collective-permute-start.10
  7.2 2.6 %collective-permute-start.11 = (bf16[256,512]{1,0:T(8,128)(2,1)}, bf16[256,512]{1,0:T(8,128)(2,1)S(1)}, u32[]{:S(2)}, u32[]{:S(2)}) collective-permute-start(bf16[256,512]{1,0:T(8,128)(2,1)} %get-tuple-element.43), channel_id=1, source_target_pairs={{0,2},{1,3},{2,0},{3,1},{4,6},{5,7},{6,4},{7,5},{8,10},{9,11},{10,... | collective-permute-start | bytes 786440 | tf_op jit(solution)/shard_map/ppermute | solution.py:344
  9.8 0.1 collective-permute-start.12
  9.9 7.1 %front.2 = (bf16[256,512]{1,0:T(8,128)(2,1)}, bf16[256,512]{1,0:T(8,128)(2,1)}, bf16[256,512]{1,0:T(8,128)(2,1)}, bf16[256,512]{1,0:T(8,128)(2,1)}) custom-call(s32[32]{0:T(128)} %occ_at.3, s32[32]{0:T(128)} %emp_at.3, bf16[8,16,4096]{2,1,0:T(8,128)(2,1)} %rest_0_.3, bf16[16,16,4096]{2,1,0:T(8,128)(2,1)} %rest_1_.3, ...), custom_call_target="tpu_custom_call" | custom-call | flops 1 | bytes 1 | tf_op jit(solution)/shard_map/front/pallas_call | solution.py:149
  17.0 0.2 collective-permute-start
  17.2 1.4 %collective-permute-start.1 = (bf16[256,512]{1,0:T(8,128)(2,1)}, bf16[256,512]{1,0:T(8,128)(2,1)S(1)}, u32[]{:S(2)}, u32[]{:S(2)}) collective-permute-start(bf16[256,512]{1,0:T(8,128)(2,1)} %get-tuple-element.31), channel_id=1, source_target_pairs={{0,2},{1,3},{2,0},{3,1},{4,6},{5,7},{6,4},{7,5},{8,10},{9,11},{10,... | collective-permute-start | bytes 786440 | tf_op jit(solution)/shard_map/ppermute | solution.py:344
  18.6 0.3 collective-permute-start.2
  18.9 0.0 collective-permute-done.11.rest_2_
  18.9 3.5 %collective-permute-done.12.rest_3_ = bf16[256,512]{1,0:T(8,128)(2,1)S(1)} collective-permute-done((bf16[256,512]{1,0:T(8,128)(2,1)}, bf16[256,512]{1,0:T(8,128)(2,1)S(1)}, u32[]{:S(2)}, u32[]{:S(2)}) %collective-permute-start.12) | collective-permute-done | bytes 262176 | tf_op jit(solution)/shard_map/ppermute | solution.py:344
  22.4 0.9 copy-done.3
  23.3 1.7 %across.3 = (bf16[128,512]{1,0:T(8,128)(2,1)S(1)}, bf16[128,512]{1,0:T(8,128)(2,1)S(1)}, bf16[128,512]{1,0:T(8,128)(2,1)S(1)}, bf16[128,512]{1,0:T(8,128)(2,1)S(...) custom-call(bf16[256,512]{1,0:T(8,128)(2,1)S(1)} %copy-done.5, ...), custom_call_target="tpu_custom_call" | custom-call | flops 1 | bytes 1 | tf_op jit(solution)/shard_map/across/pallas_call | solution.py:212
  25.0 1.6 %collective-permute-start.13 = (bf16[128,512]{1,0:T(8,128)(2,1)S(1)}, bf16[128,512]{1,0:T(8,128)(2,1)S(1)}, u32[]{:S(2)}, u32[]{:S(2)}) collective-permute-start(bf16[128,512]{1,0:T(8,128)(2,1)S(1)} %get-tuple-element.46), channel_id=1, source_target_pairs={{0,4},{4,0},{8,12},{12,8},{16,20},{20,16},{24,28},{28,24},{1,5},{5... | collective-permute-start | bytes 393224 | tf_op jit(solution)/shard_map/ppermute | solution.py:344
  26.6 1.6 %collective-permute-start.14 = (bf16[128,512]{1,0:T(8,128)(2,1)S(1)}, bf16[128,512]{1,0:T(8,128)(2,1)S(1)}, u32[]{:S(2)}, u32[]{:S(2)}) collective-permute-start(bf16[128,512]{1,0:T(8,128)(2,1)S(1)} %get-tuple-element.47), channel_id=1, source_target_pairs={{0,8},{4,12},{8,0},{12,4},{16,24},{20,28},{24,16},{28,20},{1,9},{5... | collective-permute-start | bytes 393224 | tf_op jit(solution)/shard_map/ppermute | solution.py:344
  28.2 0.0 collective-permute-done.rest_1_
  28.2 0.4 collective-permute-start.15
  28.6 2.9 %collective-permute-start.16 = (bf16[128,512]{1,0:T(8,128)(2,1)S(1)}, bf16[128,512]{1,0:T(8,128)(2,1)S(1)}, u32[]{:S(2)}, u32[]{:S(2)}) collective-permute-start(bf16[128,512]{1,0:T(8,128)(2,1)S(1)} %get-tuple-element.49), channel_id=1, source_target_pairs={{0,16},{4,20},{8,24},{12,28},{16,0},{20,4},{24,8},{28,12},{1,17},{... | collective-permute-start | bytes 393224 | tf_op jit(solution)/shard_map/ppermute | solution.py:344
  31.5 2.0 %collective-permute-done.2.rest_3_ = bf16[256,512]{1,0:T(8,128)(2,1)S(1)} collective-permute-done((bf16[256,512]{1,0:T(8,128)(2,1)}, bf16[256,512]{1,0:T(8,128)(2,1)S(1)}, u32[]{:S(2)}, u32[]{:S(2)}) %collective-permute-start.2) | collective-permute-done | bytes 262176 | tf_op jit(solution)/shard_map/ppermute | solution.py:344
  33.5 3.6 %collective-permute-start.17 = (bf16[128,512]{1,0:T(8,128)(2,1)S(1)}, bf16[128,512]{1,0:T(8,128)(2,1)S(1)}, u32[]{:S(2)}, u32[]{:S(2)}) collective-permute-start(bf16[128,512]{1,0:T(8,128)(2,1)S(1)} %get-tuple-element.50), channel_id=1, source_target_pairs={{0,20},{4,16},{8,28},{12,24},{16,4},{20,0},{24,12},{28,8},{1,21},{... | collective-permute-start | bytes 393224 | tf_op jit(solution)/shard_map/ppermute | solution.py:344
  37.1 1.7 %across.2 = (bf16[128,512]{1,0:T(8,128)(2,1)S(1)}, bf16[128,512]{1,0:T(8,128)(2,1)S(1)}, bf16[128,512]{1,0:T(8,128)(2,1)S(1)}, bf16[128,512]{1,0:T(8,128)(2,1)S(...) custom-call(bf16[256,512]{1,0:T(8,128)(2,1)S(1)} %copy-done.3, ...), custom_call_target="tpu_custom_call" | custom-call | flops 1 | bytes 1 | tf_op jit(solution)/shard_map/across/pallas_call | solution.py:212
  38.8 1.4 %collective-permute-start.18 = (bf16[128,512]{1,0:T(8,128)(2,1)S(1)}, bf16[128,512]{1,0:T(8,128)(2,1)S(1)}, u32[]{:S(2)}, u32[]{:S(2)}) collective-permute-start(bf16[128,512]{1,0:T(8,128)(2,1)S(1)} %get-tuple-element.51), channel_id=1, source_target_pairs={{0,24},{4,28},{8,16},{12,20},{16,8},{20,12},{24,0},{28,4},{1,25},{... | collective-permute-start | bytes 393224 | tf_op jit(solution)/shard_map/ppermute | solution.py:344
  40.2 0.0 collective-permute-done.14.rest_2_
  40.2 2.4 %collective-permute-start.19 = (bf16[128,512]{1,0:T(8,128)(2,1)S(1)}, bf16[128,512]{1,0:T(8,128)(2,1)S(1)}, u32[]{:S(2)}, u32[]{:S(2)}) collective-permute-start(bf16[128,512]{1,0:T(8,128)(2,1)S(1)} %get-tuple-element.52), channel_id=1, source_target_pairs={{0,28},{4,24},{8,20},{12,16},{16,12},{20,8},{24,4},{28,0},{1,29},{... | collective-permute-start | bytes 393224 | tf_op jit(solution)/shard_map/ppermute | solution.py:344
  42.6 0.0 collective-permute-done.15.rest_3_
  42.6 1.5 %collective-permute-start.3 = (bf16[128,512]{1,0:T(8,128)(2,1)S(1)}, bf16[128,512]{1,0:T(8,128)(2,1)S(1)}, u32[]{:S(2)}, u32[]{:S(2)}) collective-permute-start(bf16[128,512]{1,0:T(8,128)(2,1)S(1)} %get-tuple-element.34), channel_id=1, source_target_pairs={{0,4},{4,0},{8,12},{12,8},{16,20},{20,16},{24,28},{28,24},{1,5},{5... | collective-permute-start | bytes 393224 | tf_op jit(solution)/shard_map/ppermute | solution.py:344
  44.2 0.0 collective-permute-done.16.rest_4_
  44.2 0.0 collective-permute-start.4
  44.2 7.3 %collective-permute-done.17.rest_5_ = bf16[128,512]{1,0:T(8,128)(2,1)S(1)} collective-permute-done((bf16[128,512]{1,0:T(8,128)(2,1)S(1)}, bf16[128,512]{1,0:T(8,128)(2,1)S(1)}, u32[]{:S(2)}, u32[]{:S(2)}) %collective-permute-start.17) | collective-permute-done | bytes 131104 | tf_op jit(solution)/shard_map/ppermute | solution.py:344
  51.4 0.0 collective-permute-start.5
  51.4 0.0 collective-permute-done.18.rest_6_
  51.4 3.9 %collective-permute-start.6 = (bf16[128,512]{1,0:T(8,128)(2,1)S(1)}, bf16[128,512]{1,0:T(8,128)(2,1)S(1)}, u32[]{:S(2)}, u32[]{:S(2)}) collective-permute-start(bf16[128,512]{1,0:T(8,128)(2,1)S(1)} %get-tuple-element.37), channel_id=1, source_target_pairs={{0,16},{4,20},{8,24},{12,28},{16,0},{20,4},{24,8},{28,12},{1,17},{... | collective-permute-start | bytes 393224 | tf_op jit(solution)/shard_map/ppermute | solution.py:344
  55.4 0.0 collective-permute-done.19.rest_7_
  55.4 7.9 %collective-permute-start.7 = (bf16[128,512]{1,0:T(8,128)(2,1)S(1)}, bf16[128,512]{1,0:T(8,128)(2,1)S(1)}, u32[]{:S(2)}, u32[]{:S(2)}) collective-permute-start(bf16[128,512]{1,0:T(8,128)(2,1)S(1)} %get-tuple-element.38), channel_id=1, source_target_pairs={{0,20},{4,16},{8,28},{12,24},{16,4},{20,0},{24,12},{28,8},{1,21},{... | collective-permute-start | bytes 393224 | tf_op jit(solution)/shard_map/ppermute | solution.py:344
  63.2 1.8 %collective-permute-start.8 = (bf16[128,512]{1,0:T(8,128)(2,1)S(1)}, bf16[128,512]{1,0:T(8,128)(2,1)S(1)}, u32[]{:S(2)}, u32[]{:S(2)}) collective-permute-start(bf16[128,512]{1,0:T(8,128)(2,1)S(1)} %get-tuple-element.39), channel_id=1, source_target_pairs={{0,24},{4,28},{8,16},{12,20},{16,8},{20,12},{24,0},{28,4},{1,25},{... | collective-permute-start | bytes 393224 | tf_op jit(solution)/shard_map/ppermute | solution.py:344
  65.0 0.1 collective-permute-start.9
  65.1 0.7 project.2.rest_8_
  65.8 0.0 copy-start.6
  65.9 9.2 %collective-permute-done.7.rest_5_ = bf16[128,512]{1,0:T(8,128)(2,1)S(1)} collective-permute-done((bf16[128,512]{1,0:T(8,128)(2,1)S(1)}, bf16[128,512]{1,0:T(8,128)(2,1)S(1)}, u32[]{:S(2)}, u32[]{:S(2)}) %collective-permute-start.7) | collective-permute-done | bytes 131104 | tf_op jit(solution)/shard_map/ppermute | solution.py:344
  75.1 0.7 project.3
  75.8 19.5 %all_to_all.10 = bf16[32,32,128]{2,1,0:T(8,128)(2,1)S(1)} all-to-all(bf16[32,32,128]{2,1,0:T(8,128)(2,1)S(1)} %project.3), channel_id=1, replica_groups=mesh['wide'=8,'narrow'=4] {'wide','narrow'}, dimensions={0} | all-to-all | bytes 524288 | tf_op jit(solution)/shard_map/all_to_all | solution.py:352
  95.3 0.1 reduce_sum.12
  95.3 0.7 broadcast_in_dim.2
  96.1 2.6 %all-to-all-start.1 = ((bf16[32,32,128]{2,1,0:T(8,128)(2,1)}), bf16[32,32,128]{2,1,0:T(8,128)(2,1)S(1)}, u32[]{:S(2)}, u32[]{:S(2)}) async-start(bf16[32,32,128]{2,1,0:T(8,128)(2,1)} %broadcast_in_dim.2), calls=%async_computation.1 | async-start | bytes 524288 | tf_op jit(solution)/shard_map/all_to_all | solution.py:355
  98.7 0.3 fusion
  98.9 0.3 turn.2.rest_2_
  99.3 0.3 turn.3.rest_3_
  99.6 9.7 %all-to-all-done.1.rest_0_ = bf16[32,32,128]{2,1,0:T(8,128)(2,1)S(1)} async-done(((bf16[32,32,128]{2,1,0:T(8,128)(2,1)}), bf16[32,32,128]{2,1,0:T(8,128)(2,1)S(1)}, u32[]{:S(2)}, u32[]{:S(2)}) %all-to-all-start.1) | async-done | bytes 262176 | tf_op jit(solution)/shard_map/all_to_all | solution.py:355
  109.2 15.0 %respond.1 = bf16[8,4096,512]{2,1,0:T(8,128)(2,1)} custom-call(bf16[32,32,128]{2,1,0:T(8,128)(2,1)S(1)} %all-to-all-done.1.rest_0_, f32[8,2,16,8]{3,2,1,0:T(8,128)S(1)} %bitcast.2, bf16[4096,128]{1,0:T(8,128)(2,1)S(1)} %turn.2.rest_2_, bf16[4096,128]{1,0:T(8,128)(2,1)S(1)} %turn.3.rest_3_), custom_call_target="tpu_custom_call" | custom-call | flops 1 | bytes 1 | tf_op jit(solution)/shard_map/respond/pallas_call | solution.py:326
  (21 shorter events, 0.0 us)
Async XLA Ops:
  0.0 98.6 %copy-start = (f32[64,8]{0,1:T(8,128)S(1)}, f32[64,8]{0,1:T(8,128)}, u32[]{:S(2)}) copy-start(f32[64,8]{0,1:T(8,128)} %param.16) | copy-start | bytes 6148
  0.0 22.4 %copy-start.2 = (bf16[4,512,256]{2,1,0:T(8,128)(2,1)S(1)}, bf16[4,512,256]{2,1,0:T(8,128)(2,1)}, u32[]{:S(2)}) copy-start(bf16[4,512,256]{2,1,0:T(8,128)(2,1)} %constant.13.clone.rest_4_) | copy-start | bytes 3145732
  0.0 22.4 %copy-start.4 = (bf16[256,256]{1,0:T(8,128)(2,1)S(1)}, bf16[256,256]{1,0:T(8,128)(2,1)}, u32[]{:S(2)}) copy-start(bf16[256,256]{1,0:T(8,128)(2,1)} %constant.14.clone.rest_5_) | copy-start | bytes 393220
  6.7 15.7 %copy-start.5 = (bf16[256,512]{1,0:T(8,128)(2,1)S(1)}, bf16[256,512]{1,0:T(8,128)(2,1)}, u32[]{:S(2)}) copy-start(bf16[256,512]{1,0:T(8,128)(2,1)} %get-tuple-element.41.rest_0_) | copy-start | bytes 786436
  6.7 11.9 %collective-permute-start.10 = (bf16[256,512]{1,0:T(8,128)(2,1)}, bf16[256,512]{1,0:T(8,128)(2,1)S(1)}, u32[]{:S(2)}, u32[]{:S(2)}) collective-permute-start(bf16[256,512]{1,0:T(8,128)(2,1)} %get-tuple-element.42), channel_id=1, source_target_pairs={{0,1},{1,0},{2,3},{3,2},{4,5},{5,4},{6,7},{7,6},{8,9},{9,8},{10,11... | collective-permute-start | bytes 786440 | tf_op jit(solution)/shard_map/ppermute | solution.py:344
  7.2 11.6 %collective-permute-start.11 = (bf16[256,512]{1,0:T(8,128)(2,1)}, bf16[256,512]{1,0:T(8,128)(2,1)S(1)}, u32[]{:S(2)}, u32[]{:S(2)}) collective-permute-start(bf16[256,512]{1,0:T(8,128)(2,1)} %get-tuple-element.43), channel_id=1, source_target_pairs={{0,2},{1,3},{2,0},{3,1},{4,6},{5,7},{6,4},{7,5},{8,10},{9,11},{10,... | collective-permute-start | bytes 786440 | tf_op jit(solution)/shard_map/ppermute | solution.py:344
  9.8 55.3 %copy-start.1 = (bf16[4096,512]{1,0:T(8,128)(2,1)S(1)}, bf16[4096,512]{1,0:T(8,128)(2,1)}, u32[]{:S(2)}) copy-start(bf16[4096,512]{1,0:T(8,128)(2,1)} %trial.3) | copy-start | bytes 12582916
  9.8 12.6 %collective-permute-start.12 = (bf16[256,512]{1,0:T(8,128)(2,1)}, bf16[256,512]{1,0:T(8,128)(2,1)S(1)}, u32[]{:S(2)}, u32[]{:S(2)}) collective-permute-start(bf16[256,512]{1,0:T(8,128)(2,1)} %get-tuple-element.44), channel_id=1, source_target_pairs={{0,3},{1,2},{2,1},{3,0},{4,7},{5,6},{6,5},{7,4},{8,11},{9,10},{10,... | collective-permute-start | bytes 786440 | tf_op jit(solution)/shard_map/ppermute | solution.py:344
  17.0 11.2 %collective-permute-start = (bf16[256,512]{1,0:T(8,128)(2,1)}, bf16[256,512]{1,0:T(8,128)(2,1)S(1)}, u32[]{:S(2)}, u32[]{:S(2)}) collective-permute-start(bf16[256,512]{1,0:T(8,128)(2,1)} %get-tuple-element.30), channel_id=1, source_target_pairs={{0,1},{1,0},{2,3},{3,2},{4,5},{5,4},{6,7},{7,6},{8,9},{9,8},{10,11... | collective-permute-start | bytes 786440 | tf_op jit(solution)/shard_map/ppermute | solution.py:344
  17.2 11.4 %collective-permute-start.1 = (bf16[256,512]{1,0:T(8,128)(2,1)}, bf16[256,512]{1,0:T(8,128)(2,1)S(1)}, u32[]{:S(2)}, u32[]{:S(2)}) collective-permute-start(bf16[256,512]{1,0:T(8,128)(2,1)} %get-tuple-element.31), channel_id=1, source_target_pairs={{0,2},{1,3},{2,0},{3,1},{4,6},{5,7},{6,4},{7,5},{8,10},{9,11},{10,... | collective-permute-start | bytes 786440 | tf_op jit(solution)/shard_map/ppermute | solution.py:344
  18.6 14.9 %collective-permute-start.2 = (bf16[256,512]{1,0:T(8,128)(2,1)}, bf16[256,512]{1,0:T(8,128)(2,1)S(1)}, u32[]{:S(2)}, u32[]{:S(2)}) collective-permute-start(bf16[256,512]{1,0:T(8,128)(2,1)} %get-tuple-element.32), channel_id=1, source_target_pairs={{0,3},{1,2},{2,1},{3,0},{4,7},{5,6},{6,5},{7,4},{8,11},{9,10},{10,... | collective-permute-start | bytes 786440 | tf_op jit(solution)/shard_map/ppermute | solution.py:344
  22.4 1.0 copy-start.3
  25.0 13.8 %collective-permute-start.13 = (bf16[128,512]{1,0:T(8,128)(2,1)S(1)}, bf16[128,512]{1,0:T(8,128)(2,1)S(1)}, u32[]{:S(2)}, u32[]{:S(2)}) collective-permute-start(bf16[128,512]{1,0:T(8,128)(2,1)S(1)} %get-tuple-element.46), channel_id=1, source_target_pairs={{0,4},{4,0},{8,12},{12,8},{16,20},{20,16},{24,28},{28,24},{1,5},{5... | collective-permute-start | bytes 393224 | tf_op jit(solution)/shard_map/ppermute | solution.py:344
  26.6 13.6 %collective-permute-start.14 = (bf16[128,512]{1,0:T(8,128)(2,1)S(1)}, bf16[128,512]{1,0:T(8,128)(2,1)S(1)}, u32[]{:S(2)}, u32[]{:S(2)}) collective-permute-start(bf16[128,512]{1,0:T(8,128)(2,1)S(1)} %get-tuple-element.47), channel_id=1, source_target_pairs={{0,8},{4,12},{8,0},{12,4},{16,24},{20,28},{24,16},{28,20},{1,9},{5... | collective-permute-start | bytes 393224 | tf_op jit(solution)/shard_map/ppermute | solution.py:344
  28.2 14.5 %collective-permute-start.15 = (bf16[128,512]{1,0:T(8,128)(2,1)S(1)}, bf16[128,512]{1,0:T(8,128)(2,1)S(1)}, u32[]{:S(2)}, u32[]{:S(2)}) collective-permute-start(bf16[128,512]{1,0:T(8,128)(2,1)S(1)} %get-tuple-element.48), channel_id=1, source_target_pairs={{0,12},{4,8},{8,4},{12,0},{16,28},{20,24},{24,20},{28,16},{1,13},{... | collective-permute-start | bytes 393224 | tf_op jit(solution)/shard_map/ppermute | solution.py:344
  28.6 15.6 %collective-permute-start.16 = (bf16[128,512]{1,0:T(8,128)(2,1)S(1)}, bf16[128,512]{1,0:T(8,128)(2,1)S(1)}, u32[]{:S(2)}, u32[]{:S(2)}) collective-permute-start(bf16[128,512]{1,0:T(8,128)(2,1)S(1)} %get-tuple-element.49), channel_id=1, source_target_pairs={{0,16},{4,20},{8,24},{12,28},{16,0},{20,4},{24,8},{28,12},{1,17},{... | collective-permute-start | bytes 393224 | tf_op jit(solution)/shard_map/ppermute | solution.py:344
  33.5 17.9 %collective-permute-start.17 = (bf16[128,512]{1,0:T(8,128)(2,1)S(1)}, bf16[128,512]{1,0:T(8,128)(2,1)S(1)}, u32[]{:S(2)}, u32[]{:S(2)}) collective-permute-start(bf16[128,512]{1,0:T(8,128)(2,1)S(1)} %get-tuple-element.50), channel_id=1, source_target_pairs={{0,20},{4,16},{8,28},{12,24},{16,4},{20,0},{24,12},{28,8},{1,21},{... | collective-permute-start | bytes 393224 | tf_op jit(solution)/shard_map/ppermute | solution.py:344
  38.8 12.6 %collective-permute-start.18 = (bf16[128,512]{1,0:T(8,128)(2,1)S(1)}, bf16[128,512]{1,0:T(8,128)(2,1)S(1)}, u32[]{:S(2)}, u32[]{:S(2)}) collective-permute-start(bf16[128,512]{1,0:T(8,128)(2,1)S(1)} %get-tuple-element.51), channel_id=1, source_target_pairs={{0,24},{4,28},{8,16},{12,20},{16,8},{20,12},{24,0},{28,4},{1,25},{... | collective-permute-start | bytes 393224 | tf_op jit(solution)/shard_map/ppermute | solution.py:344
  40.2 15.1 %collective-permute-start.19 = (bf16[128,512]{1,0:T(8,128)(2,1)S(1)}, bf16[128,512]{1,0:T(8,128)(2,1)S(1)}, u32[]{:S(2)}, u32[]{:S(2)}) collective-permute-start(bf16[128,512]{1,0:T(8,128)(2,1)S(1)} %get-tuple-element.52), channel_id=1, source_target_pairs={{0,28},{4,24},{8,20},{12,16},{16,12},{20,8},{24,4},{28,0},{1,29},{... | collective-permute-start | bytes 393224 | tf_op jit(solution)/shard_map/ppermute | solution.py:344
  42.6 20.6 %collective-permute-start.3 = (bf16[128,512]{1,0:T(8,128)(2,1)S(1)}, bf16[128,512]{1,0:T(8,128)(2,1)S(1)}, u32[]{:S(2)}, u32[]{:S(2)}) collective-permute-start(bf16[128,512]{1,0:T(8,128)(2,1)S(1)} %get-tuple-element.34), channel_id=1, source_target_pairs={{0,4},{4,0},{8,12},{12,8},{16,20},{20,16},{24,28},{28,24},{1,5},{5... | collective-permute-start | bytes 393224 | tf_op jit(solution)/shard_map/ppermute | solution.py:344
  44.2 20.9 %collective-permute-start.4 = (bf16[128,512]{1,0:T(8,128)(2,1)S(1)}, bf16[128,512]{1,0:T(8,128)(2,1)S(1)}, u32[]{:S(2)}, u32[]{:S(2)}) collective-permute-start(bf16[128,512]{1,0:T(8,128)(2,1)S(1)} %get-tuple-element.35), channel_id=1, source_target_pairs={{0,8},{4,12},{8,0},{12,4},{16,24},{20,28},{24,16},{28,20},{1,9},{5... | collective-permute-start | bytes 393224 | tf_op jit(solution)/shard_map/ppermute | solution.py:344
  51.4 14.4 %collective-permute-start.5 = (bf16[128,512]{1,0:T(8,128)(2,1)S(1)}, bf16[128,512]{1,0:T(8,128)(2,1)S(1)}, u32[]{:S(2)}, u32[]{:S(2)}) collective-permute-start(bf16[128,512]{1,0:T(8,128)(2,1)S(1)} %get-tuple-element.36), channel_id=1, source_target_pairs={{0,12},{4,8},{8,4},{12,0},{16,28},{20,24},{24,20},{28,16},{1,13},{... | collective-permute-start | bytes 393224 | tf_op jit(solution)/shard_map/ppermute | solution.py:344
  51.4 14.4 %collective-permute-start.6 = (bf16[128,512]{1,0:T(8,128)(2,1)S(1)}, bf16[128,512]{1,0:T(8,128)(2,1)S(1)}, u32[]{:S(2)}, u32[]{:S(2)}) collective-permute-start(bf16[128,512]{1,0:T(8,128)(2,1)S(1)} %get-tuple-element.37), channel_id=1, source_target_pairs={{0,16},{4,20},{8,24},{12,28},{16,0},{20,4},{24,8},{28,12},{1,17},{... | collective-permute-start | bytes 393224 | tf_op jit(solution)/shard_map/ppermute | solution.py:344
  55.4 19.7 %collective-permute-start.7 = (bf16[128,512]{1,0:T(8,128)(2,1)S(1)}, bf16[128,512]{1,0:T(8,128)(2,1)S(1)}, u32[]{:S(2)}, u32[]{:S(2)}) collective-permute-start(bf16[128,512]{1,0:T(8,128)(2,1)S(1)} %get-tuple-element.38), channel_id=1, source_target_pairs={{0,20},{4,16},{8,28},{12,24},{16,4},{20,0},{24,12},{28,8},{1,21},{... | collective-permute-start | bytes 393224 | tf_op jit(solution)/shard_map/ppermute | solution.py:344
  63.2 11.8 %collective-permute-start.8 = (bf16[128,512]{1,0:T(8,128)(2,1)S(1)}, bf16[128,512]{1,0:T(8,128)(2,1)S(1)}, u32[]{:S(2)}, u32[]{:S(2)}) collective-permute-start(bf16[128,512]{1,0:T(8,128)(2,1)S(1)} %get-tuple-element.39), channel_id=1, source_target_pairs={{0,24},{4,28},{8,16},{12,20},{16,8},{20,12},{24,0},{28,4},{1,25},{... | collective-permute-start | bytes 393224 | tf_op jit(solution)/shard_map/ppermute | solution.py:344
  65.0 10.0 %collective-permute-start.9 = (bf16[128,512]{1,0:T(8,128)(2,1)S(1)}, bf16[128,512]{1,0:T(8,128)(2,1)S(1)}, u32[]{:S(2)}, u32[]{:S(2)}) collective-permute-start(bf16[128,512]{1,0:T(8,128)(2,1)S(1)} %get-tuple-element.40), channel_id=1, source_target_pairs={{0,28},{4,24},{8,20},{12,16},{16,12},{20,8},{24,4},{28,0},{1,29},{... | collective-permute-start | bytes 393224 | tf_op jit(solution)/shard_map/ppermute | solution.py:344
  65.8 32.8 %copy-start.6 = (s32[256]{0:T(256)S(1)}, s32[256]{0:T(256)}, u32[]{:S(2)}) copy-start(s32[256]{0:T(256)} %param.15) | copy-start | bytes 3076
  96.1 13.2 %all-to-all-start.1 = ((bf16[32,32,128]{2,1,0:T(8,128)(2,1)}), bf16[32,32,128]{2,1,0:T(8,128)(2,1)S(1)}, u32[]{:S(2)}, u32[]{:S(2)}) async-start(bf16[32,32,128]{2,1,0:T(8,128)(2,1)} %broadcast_in_dim.2), calls=%async_computation.1 | async-start | bytes 524288 | tf_op jit(solution)/shard_map/all_to_all | solution.py:355

commit v2 on v1

--- a/solution.py
+++ b/solution.py
@@ -12,7 +12,6 @@
 GROUP = 16
 LANES = 128
 SPLITS = ((1,), (1,))
-WHOLE = ((False,), (False,))
 PERMUTE_MOST = 8
 MIB = 1024 * 1024
 COST = pl.CostEstimate(flops=1, bytes_accessed=1, transcendentals=0)
@@ -115,12 +114,13 @@
     mats[1].start()
     places = partners(slabs, 1)
     outs = views(outs, places, 0, slabs)
+    chosen = [(occ_at[start + p], emp_at[start + p]) for p in range(GROUP)]
     for g in range(steps):
         lanes = slice(g * width, (g + 1) * width)
         pieces[g][0].wait()
         pieces[g][1].wait()
         for p in range(GROUP):
-            o, e = occ_at[start + p], emp_at[start + p]
+            o, e = chosen[p]
             prod[p * planes : (p + 1) * planes, :] = (
                 occ[o, :, lanes].astype(F32) * emp[e, :, lanes].astype(F32)
             ).astype(BF16)
@@ -165,25 +165,28 @@
     return [outs[h * each : (h + 1) * each] for h in range(len(widths))]
 
 
-def across_kernel(slabs, blocks, first, grid, taken, after, *rest):
+def across_kernel(slabs, blocks, first, grid, part, taken, after, *rest):
     places = partners(slabs, blocks)
     parts = views(rest[:taken], places, 0, slabs)
     xmat, swap = rest[taken : taken + 2]
     outs, whole = views(rest[taken + 2 + after : -1], places, slabs, blocks), rest[-1]
+    count = whole.shape[0]
+    half = 0 if part is None else places[slabs] // count ^ part
+    tall = grid // blocks * count
     rows, wide = parts[0].shape
     planes = rows // GROUP
-    half = grid // 2
-    channels = 2 * (half // slabs)
-    lane = first + lax.broadcasted_iota(jnp.int32, (grid, wide), 1)
-    kx = lax.broadcasted_iota(jnp.int32, (grid, wide), 0)
-    kx = jnp.where(kx < half, kx, kx - grid)
+    channels = grid // slabs
+    lane = first + lax.broadcasted_iota(jnp.int32, (tall, wide), 1)
+    kx = half * tall + lax.broadcasted_iota(jnp.int32, (tall, wide), 0)
+    kx = jnp.where(kx < grid // 2, kx, kx - grid)
     ky = lane // channels
-    ky = jnp.where(ky < half // 2, ky, ky - half)
+    ky = jnp.where(ky < grid // 4, ky, ky - grid // 2)
     kz = places[0] * (channels // 2) + lane % channels // 2
     squared = (kx * kx + ky * ky + kz * kz).astype(F32)
     quarter = float(grid // 4)
     coulomb = (1.0 / jnp.sqrt(1.0 + squared / (quarter * quarter)))[:, None, :]
-    left = jnp.concatenate([xmat[places[s]] for s in range(slabs)], axis=1)
+    rows_here = pl.ds(half * (8 * tall), 8 * tall)
+    left = jnp.concatenate([xmat[places[s], rows_here, :] for s in range(slabs)], axis=1)
     found = []
     for m in range(GROUP // 8):
         right = []
@@ -197,25 +200,27 @@
             right.append(jnp.concatenate(turned, axis=1).astype(BF16))
         right = jnp.concatenate(right, axis=0)
         total = jnp.dot(left, right, preferred_element_type=F32)
-        found.append(total.reshape(grid, 8, wide) * coulomb)
+        found.append(total.reshape(tall, 8, wide) * coulomb)
     found = jnp.concatenate(found, axis=1).astype(BF16)
     whole[...] = found.reshape(whole.shape)
-    for s in range(blocks):
-        outs[s][...] = whole[places[slabs + s]]
-
-
-def across(slabs, blocks, first, grid, parts, xmat, swap, whole, after):
+    for i in range(count):
+        at = places[slabs + (part or 0) * count + i]
+        outs[i][...] = whole[at - half * count]
+
+
+def across(slabs, blocks, first, grid, parts, xmat, swap, part, after):
     rows, wide = parts[0].shape[-2:]
     tall = grid // blocks * GROUP
-    out_shape = shapes(blocks, tall, wide, whole)
+    count = blocks if part is None else blocks // 2
+    out_shape = shapes(count, tall, wide, part is None)
     vmem = pl.BlockSpec(memory_space=pltpu.VMEM)
     return pl.pallas_call(
-        functools.partial(across_kernel, slabs, blocks, first, grid, len(parts), len(after)),
+        functools.partial(across_kernel, slabs, blocks, first, grid, part, len(parts), len(after)),
         out_shape=out_shape,
         in_specs=[vmem] * (len(parts) + 2)
         + [pl.BlockSpec(memory_space=pl.ANY)] * len(after),
         out_specs=[vmem] * len(out_shape),
-        scratch_shapes=[pltpu.VMEM((blocks, tall, wide), BF16)],
+        scratch_shapes=[pltpu.VMEM((count, tall, wide), BF16)],
         compiler_params=pltpu.CompilerParams(vmem_limit_bytes=24 * MIB),
         cost_estimate=COST,
         name="across",
@@ -378,11 +383,15 @@
     for g in range(groups):
         first, waves[g] = 0, []
         after = [blocked[0] for blocked in sent[g + 1][1]] if g + 1 < groups else []
-        for whole, wide, blocked in zip(WHOLE[g % len(WHOLE)], *sent[g]):
+        for wide, blocked in zip(*sent[g]):
             got = exchange(blocked, "narrow")
-            waves[g].append(
-                across(slabs, blocks, first, grid, got, xmat, swap, whole, after)
-            )
+            if blocks > PERMUTE_MOST:
+                stack = across(slabs, blocks, first, grid, got, xmat, swap, None, after)
+                waves[g].append(stack)
+            else:
+                far = across(slabs, blocks, first, grid, got, xmat, swap, 1, after)
+                near = across(slabs, blocks, first, grid, got, xmat, swap, 0, far[:1])
+                waves[g].append(list(near) + list(far))
             first += wide
     shares, turned = [], []
     for g in range(groups):

time: 125 us -> 123 us (0.984)
  blocking collectives: 19.5 us -> 14.4 us
  starting transfers between devices: 36.8 us -> 38.5 us
    all_to_all x1, blocking collectives: 19.5 us -> 14.4 us  [sum_shares(): taken = lax.all_to_all(shares, both, 0, 0, tiled=True)]
    ppermute x20, starting transfers between devices: 34.2 us -> 35.9 us  [exchange(): lax.ppermute(blocks[s], axis, [(i, i ^ s) for i in range(len(blocks))])]
    pallas_call x2 -> x4, Pallas kernels: 3.31 us -> 4.23 us  [across(): pl.pallas_call(functools.partial(across_kernel, slabs, blocks, first, gri...]
  transfers between devices with their start and end apart: 21 -> 21, of which waited for: 5 -> 6; matrix products, arithmetic and copies ran while one was open for 0% -> 0% of each run, Pallas kernels for 9% -> 10%
where the time goes in v2:
time: 123 us
  starting transfers between devices  38.5 us (31%)
  Pallas kernels  34.7 us (28%)
  waiting for transfers between devices  32.8 us (27%)
  blocking collectives  14.4 us (12%)
  local copies, waits for them, and re-layouts  1.72 us (1%)
    ppermute x20, starting transfers between devices, exchange(): lax.ppermute(blocks[s], axis, [(i, i ^ s) for i in range(len(blocks))])  35.9 us
    ppermute x20, waiting for transfers between devices, exchange(): lax.ppermute(blocks[s], axis, [(i, i ^ s) for i in range(len(blocks))])  23.2 us
    pallas_call x1, Pallas kernels, respond(): pl.pallas_call(functools.partial(respond_kernel, blocks, slabs, groups, f...  15 us
    all_to_all x1, blocking collectives, sum_shares(): taken = lax.all_to_all(shares, both, 0, 0, tiled=True)  14.4 us
    pallas_call x2, Pallas kernels, front(): pl.pallas_call(functools.partial(front_kernel, start, slabs, widths), out...  13.4 us
    all_to_all x1, waiting for transfers between devices, sum_shares(): return lax.all_to_all(spread, both, 0, 0, tiled=True)  9.66 us
    pallas_call x4, Pallas kernels, across(): pl.pallas_call(functools.partial(across_kernel, slabs, blocks, first, gri...  4.23 us
    all_to_all x1, starting transfers between devices, sum_shares(): return lax.all_to_all(spread, both, 0, 0, tiled=True)  2.59 us
  transfers between devices with their start and end apart: 21, of which 6 were waited for; matrix products, arithmetic and copies ran while one was open for 0% of the time, Pallas kernels for 10%

profile of v2, /device:TPU:0, one launch (start us, length us, event | category | flops | bytes accessed | tf_op | source)
XLA Modules:
  0.0 122.6 jit_solution(16613120398925730304)
XLA Ops:
  0.0 6.7 %front.2 = (bf16[256,512]{1,0:T(8,128)(2,1)}, bf16[256,512]{1,0:T(8,128)(2,1)}, bf16[256,512]{1,0:T(8,128)(2,1)}, bf16[256,512]{1,0:T(8,128)(2,1)}) custom-call(s32[32]{0:T(128)} %occ_at.3, s32[32]{0:T(128)} %emp_at.3, bf16[8,16,4096]{2,1,0:T(8,128)(2,1)} %rest_0_.3, bf16[16,16,4096]{2,1,0:T(8,128)(2,1)} %rest_1_.3, ...), custom_call_target="tpu_custom_call" | custom-call | flops 1 | bytes 1 | tf_op jit(solution)/shard_map/front/pallas_call | solution.py:149
  6.8 0.0 copy-start.3
  6.8 0.5 collective-permute-start
  7.3 2.6 %collective-permute-start.1 = (bf16[256,512]{1,0:T(8,128)(2,1)}, bf16[256,512]{1,0:T(8,128)(2,1)S(1)}, u32[]{:S(2)}, u32[]{:S(2)}) collective-permute-start(bf16[256,512]{1,0:T(8,128)(2,1)} %get-tuple-element.31), channel_id=1, source_target_pairs={{0,2},{1,3},{2,0},{3,1},{4,6},{5,7},{6,4},{7,5},{8,10},{9,11},{10,... | collective-permute-start | bytes 786440 | tf_op jit(solution)/shard_map/ppermute | solution.py:349
  9.8 0.1 collective-permute-start.2
  9.9 6.6 %front.3 = (bf16[256,512]{1,0:T(8,128)(2,1)}, bf16[256,512]{1,0:T(8,128)(2,1)}, bf16[256,512]{1,0:T(8,128)(2,1)}, bf16[256,512]{1,0:T(8,128)(2,1)}) custom-call(s32[32]{0:T(128)} %occ_at.3, s32[32]{0:T(128)} %emp_at.3, bf16[8,16,4096]{2,1,0:T(8,128)(2,1)} %rest_0_.3, bf16[16,16,4096]{2,1,0:T(8,128)(2,1)} %rest_1_.3, ...), custom_call_target="tpu_custom_call" | custom-call | flops 1 | bytes 1 | tf_op jit(solution)/shard_map/front/pallas_call | solution.py:149
  16.5 0.2 collective-permute-start.10
  16.8 1.9 %collective-permute-start.11 = (bf16[256,512]{1,0:T(8,128)(2,1)}, bf16[256,512]{1,0:T(8,128)(2,1)S(1)}, u32[]{:S(2)}, u32[]{:S(2)}) collective-permute-start(bf16[256,512]{1,0:T(8,128)(2,1)} %get-tuple-element.43), channel_id=1, source_target_pairs={{0,2},{1,3},{2,0},{3,1},{4,6},{5,7},{6,4},{7,5},{8,10},{9,11},{10,... | collective-permute-start | bytes 786440 | tf_op jit(solution)/shard_map/ppermute | solution.py:349
  18.7 0.0 collective-permute-done.1.rest_2_
  18.7 3.7 %collective-permute-done.2.rest_3_ = bf16[256,512]{1,0:T(8,128)(2,1)S(1)} collective-permute-done((bf16[256,512]{1,0:T(8,128)(2,1)}, bf16[256,512]{1,0:T(8,128)(2,1)S(1)}, u32[]{:S(2)}, u32[]{:S(2)}) %collective-permute-start.2) | collective-permute-done | bytes 262176 | tf_op jit(solution)/shard_map/ppermute | solution.py:349
  22.4 1.1 across.4
  23.5 3.6 %collective-permute-start.7 = (bf16[128,512]{1,0:T(8,128)(2,1)S(1)}, bf16[128,512]{1,0:T(8,128)(2,1)S(1)}, u32[]{:S(2)}, u32[]{:S(2)}) collective-permute-start(bf16[128,512]{1,0:T(8,128)(2,1)S(1)} %get-tuple-element.38), channel_id=1, source_target_pairs={{0,20},{4,16},{8,28},{12,24},{16,4},{20,0},{24,12},{28,8},{1,21},{... | collective-permute-start | bytes 393224 | tf_op jit(solution)/shard_map/ppermute | solution.py:349
  27.1 1.3 %collective-permute-start.8 = (bf16[128,512]{1,0:T(8,128)(2,1)S(1)}, bf16[128,512]{1,0:T(8,128)(2,1)S(1)}, u32[]{:S(2)}, u32[]{:S(2)}) collective-permute-start(bf16[128,512]{1,0:T(8,128)(2,1)S(1)} %get-tuple-element.39), channel_id=1, source_target_pairs={{0,24},{4,28},{8,16},{12,20},{16,8},{20,12},{24,0},{28,4},{1,25},{... | collective-permute-start | bytes 393224 | tf_op jit(solution)/shard_map/ppermute | solution.py:349
  28.4 5.1 %collective-permute-done.12.rest_3_ = bf16[256,512]{1,0:T(8,128)(2,1)S(1)} collective-permute-done((bf16[256,512]{1,0:T(8,128)(2,1)}, bf16[256,512]{1,0:T(8,128)(2,1)S(1)}, u32[]{:S(2)}, u32[]{:S(2)}) %collective-permute-start.12) | collective-permute-done | bytes 262176 | tf_op jit(solution)/shard_map/ppermute | solution.py:349
  33.5 0.9 copy-done.5
  34.5 1.1 across.6
  35.5 3.7 %collective-permute-start.17 = (bf16[128,512]{1,0:T(8,128)(2,1)S(1)}, bf16[128,512]{1,0:T(8,128)(2,1)S(1)}, u32[]{:S(2)}, u32[]{:S(2)}) collective-permute-start(bf16[128,512]{1,0:T(8,128)(2,1)S(1)} %get-tuple-element.50), channel_id=1, source_target_pairs={{0,20},{4,16},{8,28},{12,24},{16,4},{20,0},{24,12},{28,8},{1,21},{... | collective-permute-start | bytes 393224 | tf_op jit(solution)/shard_map/ppermute | solution.py:349
  39.3 1.3 %collective-permute-start.18 = (bf16[128,512]{1,0:T(8,128)(2,1)S(1)}, bf16[128,512]{1,0:T(8,128)(2,1)S(1)}, u32[]{:S(2)}, u32[]{:S(2)}) collective-permute-start(bf16[128,512]{1,0:T(8,128)(2,1)S(1)} %get-tuple-element.51), channel_id=1, source_target_pairs={{0,24},{4,28},{8,16},{12,20},{16,8},{20,12},{24,0},{28,4},{1,25},{... | collective-permute-start | bytes 393224 | tf_op jit(solution)/shard_map/ppermute | solution.py:349
  40.6 2.5 %collective-permute-start.19 = (bf16[128,512]{1,0:T(8,128)(2,1)S(1)}, bf16[128,512]{1,0:T(8,128)(2,1)S(1)}, u32[]{:S(2)}, u32[]{:S(2)}) collective-permute-start(bf16[128,512]{1,0:T(8,128)(2,1)S(1)} %get-tuple-element.52), channel_id=1, source_target_pairs={{0,28},{4,24},{8,20},{12,16},{16,12},{20,8},{24,4},{28,0},{1,29},{... | collective-permute-start | bytes 393224 | tf_op jit(solution)/shard_map/ppermute | solution.py:349
  43.0 1.1 across.7
  44.1 1.6 %collective-permute-start.13 = (bf16[128,512]{1,0:T(8,128)(2,1)S(1)}, bf16[128,512]{1,0:T(8,128)(2,1)S(1)}, u32[]{:S(2)}, u32[]{:S(2)}) collective-permute-start(bf16[128,512]{1,0:T(8,128)(2,1)S(1)} %get-tuple-element.47), channel_id=1, source_target_pairs={{0,4},{4,0},{8,12},{12,8},{16,20},{20,16},{24,28},{28,24},{1,5},{5... | collective-permute-start | bytes 393224 | tf_op jit(solution)/shard_map/ppermute | solution.py:349
  45.7 6.5 %collective-permute-done.17.rest_5_ = bf16[128,512]{1,0:T(8,128)(2,1)S(1)} collective-permute-done((bf16[128,512]{1,0:T(8,128)(2,1)S(1)}, bf16[128,512]{1,0:T(8,128)(2,1)S(1)}, u32[]{:S(2)}, u32[]{:S(2)}) %collective-permute-start.17) | collective-permute-done | bytes 131104 | tf_op jit(solution)/shard_map/ppermute | solution.py:349
  52.2 0.2 collective-permute-start.15
  52.4 0.0 collective-permute-done.18.rest_6_
  52.4 4.8 %collective-permute-start.16 = (bf16[128,512]{1,0:T(8,128)(2,1)S(1)}, bf16[128,512]{1,0:T(8,128)(2,1)S(1)}, u32[]{:S(2)}, u32[]{:S(2)}) collective-permute-start(bf16[128,512]{1,0:T(8,128)(2,1)S(1)} %get-tuple-element.45.rest_6_), channel_id=1, source_target_pairs={{0,16},{4,20},{8,24},{12,28},{16,0},{20,4},{24,8},{28,12},{1,17},{... | collective-permute-start | bytes 393224 | tf_op jit(solution)/shard_map/ppermute | solution.py:349
  57.2 1.1 across.5
  58.3 0.8 collective-permute-start.9
  59.1 1.6 %collective-permute-start.3 = (bf16[128,512]{1,0:T(8,128)(2,1)S(1)}, bf16[128,512]{1,0:T(8,128)(2,1)S(1)}, u32[]{:S(2)}, u32[]{:S(2)}) collective-permute-start(bf16[128,512]{1,0:T(8,128)(2,1)S(1)} %get-tuple-element.35), channel_id=1, source_target_pairs={{0,4},{4,0},{8,12},{12,8},{16,20},{20,16},{24,28},{28,24},{1,5},{5... | collective-permute-start | bytes 393224 | tf_op jit(solution)/shard_map/ppermute | solution.py:349
  60.6 0.0 collective-permute-done.14.rest_2_
  60.6 7.8 %collective-permute-start.4 = (bf16[128,512]{1,0:T(8,128)(2,1)S(1)}, bf16[128,512]{1,0:T(8,128)(2,1)S(1)}, u32[]{:S(2)}, u32[]{:S(2)}) collective-permute-start(bf16[128,512]{1,0:T(8,128)(2,1)S(1)} %get-tuple-element.36), channel_id=1, source_target_pairs={{0,8},{4,12},{8,0},{12,4},{16,24},{20,28},{24,16},{28,20},{1,9},{5... | collective-permute-start | bytes 393224 | tf_op jit(solution)/shard_map/ppermute | solution.py:349
  68.4 0.0 collective-permute-done.15.rest_3_
  68.4 1.5 %collective-permute-start.5 = (bf16[128,512]{1,0:T(8,128)(2,1)S(1)}, bf16[128,512]{1,0:T(8,128)(2,1)S(1)}, u32[]{:S(2)}, u32[]{:S(2)}) collective-permute-start(bf16[128,512]{1,0:T(8,128)(2,1)S(1)} %get-tuple-element.37), channel_id=1, source_target_pairs={{0,12},{4,8},{8,4},{12,0},{16,28},{20,24},{24,20},{28,16},{1,13},{... | collective-permute-start | bytes 393224 | tf_op jit(solution)/shard_map/ppermute | solution.py:349
  69.9 0.0 collective-permute-start.6
  69.9 0.7 project.2.rest_8_
  70.6 0.0 copy-start.6
  70.7 0.0 collective-permute-done.3.rest_1_
  70.7 1.7 %collective-permute-done.4.rest_2_ = bf16[128,512]{1,0:T(8,128)(2,1)S(1)} collective-permute-done((bf16[128,512]{1,0:T(8,128)(2,1)S(1)}, bf16[128,512]{1,0:T(8,128)(2,1)S(1)}, u32[]{:S(2)}, u32[]{:S(2)}) %collective-permute-start.4) | collective-permute-done | bytes 131104 | tf_op jit(solution)/shard_map/ppermute | solution.py:349
  72.4 6.2 %collective-permute-done.5.rest_3_ = bf16[128,512]{1,0:T(8,128)(2,1)S(1)} collective-permute-done((bf16[128,512]{1,0:T(8,128)(2,1)S(1)}, bf16[128,512]{1,0:T(8,128)(2,1)S(1)}, u32[]{:S(2)}, u32[]{:S(2)}) %collective-permute-start.5) | collective-permute-done | bytes 131104 | tf_op jit(solution)/shard_map/ppermute | solution.py:349
  78.5 0.7 project.3
  79.2 14.4 %all_to_all.10 = bf16[32,32,128]{2,1,0:T(8,128)(2,1)S(1)} all-to-all(bf16[32,32,128]{2,1,0:T(8,128)(2,1)S(1)} %project.3), channel_id=1, replica_groups=mesh['wide'=8,'narrow'=4] {'wide','narrow'}, dimensions={0} | all-to-all | bytes 524288 | tf_op jit(solution)/shard_map/all_to_all | solution.py:357
  93.6 0.1 reduce_sum.12
  93.7 0.7 broadcast_in_dim.2
  94.4 2.6 %all-to-all-start.1 = ((bf16[32,32,128]{2,1,0:T(8,128)(2,1)}), bf16[32,32,128]{2,1,0:T(8,128)(2,1)S(1)}, u32[]{:S(2)}, u32[]{:S(2)}) async-start(bf16[32,32,128]{2,1,0:T(8,128)(2,1)} %broadcast_in_dim.2), calls=%async_computation.1 | async-start | bytes 524288 | tf_op jit(solution)/shard_map/all_to_all | solution.py:360
  97.0 0.3 fusion
  97.3 0.3 turn.2.rest_2_
  97.6 0.3 turn.3.rest_3_
  97.9 9.7 %all-to-all-done.1.rest_0_ = bf16[32,32,128]{2,1,0:T(8,128)(2,1)S(1)} async-done(((bf16[32,32,128]{2,1,0:T(8,128)(2,1)}), bf16[32,32,128]{2,1,0:T(8,128)(2,1)S(1)}, u32[]{:S(2)}, u32[]{:S(2)}) %all-to-all-start.1) | async-done | bytes 262176 | tf_op jit(solution)/shard_map/all_to_all | solution.py:360
  107.6 15.0 %respond.1 = bf16[8,4096,512]{2,1,0:T(8,128)(2,1)} custom-call(bf16[32,32,128]{2,1,0:T(8,128)(2,1)S(1)} %all-to-all-done.1.rest_0_, f32[8,2,16,8]{3,2,1,0:T(8,128)S(1)} %bitcast.2, bf16[4096,128]{1,0:T(8,128)(2,1)S(1)} %turn.2.rest_2_, bf16[4096,128]{1,0:T(8,128)(2,1)S(1)} %turn.3.rest_3_), custom_call_target="tpu_custom_call" | custom-call | flops 1 | bytes 1 | tf_op jit(solution)/shard_map/respond/pallas_call | solution.py:331
  (23 shorter events, 0.1 us)
Async XLA Ops:
  0.0 97.0 %copy-start = (f32[64,8]{0,1:T(8,128)S(1)}, f32[64,8]{0,1:T(8,128)}, u32[]{:S(2)}) copy-start(f32[64,8]{0,1:T(8,128)} %param.16) | copy-start | bytes 6148
  0.0 22.4 %copy-start.2 = (bf16[4,512,256]{2,1,0:T(8,128)(2,1)S(1)}, bf16[4,512,256]{2,1,0:T(8,128)(2,1)}, u32[]{:S(2)}) copy-start(bf16[4,512,256]{2,1,0:T(8,128)(2,1)} %constant.13.clone.rest_4_) | copy-start | bytes 3145732
  0.0 22.4 %copy-start.4 = (bf16[256,256]{1,0:T(8,128)(2,1)S(1)}, bf16[256,256]{1,0:T(8,128)(2,1)}, u32[]{:S(2)}) copy-start(bf16[256,256]{1,0:T(8,128)(2,1)} %constant.14.clone.rest_5_) | copy-start | bytes 393220
  6.8 15.6 %copy-start.3 = (bf16[256,512]{1,0:T(8,128)(2,1)S(1)}, bf16[256,512]{1,0:T(8,128)(2,1)}, u32[]{:S(2)}) copy-start(bf16[256,512]{1,0:T(8,128)(2,1)} %get-tuple-element.29.rest_0_.rest_6_) | copy-start | bytes 786436
  6.8 11.9 %collective-permute-start = (bf16[256,512]{1,0:T(8,128)(2,1)}, bf16[256,512]{1,0:T(8,128)(2,1)S(1)}, u32[]{:S(2)}, u32[]{:S(2)}) collective-permute-start(bf16[256,512]{1,0:T(8,128)(2,1)} %get-tuple-element.30), channel_id=1, source_target_pairs={{0,1},{1,0},{2,3},{3,2},{4,5},{5,4},{6,7},{7,6},{8,9},{9,8},{10,11... | collective-permute-start | bytes 786440 | tf_op jit(solution)/shard_map/ppermute | solution.py:349
  7.3 11.4 %collective-permute-start.1 = (bf16[256,512]{1,0:T(8,128)(2,1)}, bf16[256,512]{1,0:T(8,128)(2,1)S(1)}, u32[]{:S(2)}, u32[]{:S(2)}) collective-permute-start(bf16[256,512]{1,0:T(8,128)(2,1)} %get-tuple-element.31), channel_id=1, source_target_pairs={{0,2},{1,3},{2,0},{3,1},{4,6},{5,7},{6,4},{7,5},{8,10},{9,11},{10,... | collective-permute-start | bytes 786440 | tf_op jit(solution)/shard_map/ppermute | solution.py:349
  9.8 12.6 %collective-permute-start.2 = (bf16[256,512]{1,0:T(8,128)(2,1)}, bf16[256,512]{1,0:T(8,128)(2,1)S(1)}, u32[]{:S(2)}, u32[]{:S(2)}) collective-permute-start(bf16[256,512]{1,0:T(8,128)(2,1)} %get-tuple-element.32), channel_id=1, source_target_pairs={{0,3},{1,2},{2,1},{3,0},{4,7},{5,6},{6,5},{7,4},{8,11},{9,10},{10,... | collective-permute-start | bytes 786440 | tf_op jit(solution)/shard_map/ppermute | solution.py:349
  16.5 11.9 %collective-permute-start.10 = (bf16[256,512]{1,0:T(8,128)(2,1)}, bf16[256,512]{1,0:T(8,128)(2,1)S(1)}, u32[]{:S(2)}, u32[]{:S(2)}) collective-permute-start(bf16[256,512]{1,0:T(8,128)(2,1)} %get-tuple-element.42), channel_id=1, source_target_pairs={{0,1},{1,0},{2,3},{3,2},{4,5},{5,4},{6,7},{7,6},{8,9},{9,8},{10,11... | collective-permute-start | bytes 786440 | tf_op jit(solution)/shard_map/ppermute | solution.py:349
  16.8 11.7 %collective-permute-start.11 = (bf16[256,512]{1,0:T(8,128)(2,1)}, bf16[256,512]{1,0:T(8,128)(2,1)S(1)}, u32[]{:S(2)}, u32[]{:S(2)}) collective-permute-start(bf16[256,512]{1,0:T(8,128)(2,1)} %get-tuple-element.43), channel_id=1, source_target_pairs={{0,2},{1,3},{2,0},{3,1},{4,6},{5,7},{6,4},{7,5},{8,10},{9,11},{10,... | collective-permute-start | bytes 786440 | tf_op jit(solution)/shard_map/ppermute | solution.py:349
  18.7 14.8 %collective-permute-start.12 = (bf16[256,512]{1,0:T(8,128)(2,1)}, bf16[256,512]{1,0:T(8,128)(2,1)S(1)}, u32[]{:S(2)}, u32[]{:S(2)}) collective-permute-start(bf16[256,512]{1,0:T(8,128)(2,1)} %get-tuple-element.44), channel_id=1, source_target_pairs={{0,3},{1,2},{2,1},{3,0},{4,7},{5,6},{6,5},{7,4},{8,11},{9,10},{10,... | collective-permute-start | bytes 786440 | tf_op jit(solution)/shard_map/ppermute | solution.py:349
  22.4 47.5 %copy-start.1 = (bf16[4096,512]{1,0:T(8,128)(2,1)S(1)}, bf16[4096,512]{1,0:T(8,128)(2,1)}, u32[]{:S(2)}) copy-start(bf16[4096,512]{1,0:T(8,128)(2,1)} %trial.3) | copy-start | bytes 12582916
  23.5 20.6 %collective-permute-start.7 = (bf16[128,512]{1,0:T(8,128)(2,1)S(1)}, bf16[128,512]{1,0:T(8,128)(2,1)S(1)}, u32[]{:S(2)}, u32[]{:S(2)}) collective-permute-start(bf16[128,512]{1,0:T(8,128)(2,1)S(1)} %get-tuple-element.38), channel_id=1, source_target_pairs={{0,20},{4,16},{8,28},{12,24},{16,4},{20,0},{24,12},{28,8},{1,21},{... | collective-permute-start | bytes 393224 | tf_op jit(solution)/shard_map/ppermute | solution.py:349
  27.1 18.6 %collective-permute-start.8 = (bf16[128,512]{1,0:T(8,128)(2,1)S(1)}, bf16[128,512]{1,0:T(8,128)(2,1)S(1)}, u32[]{:S(2)}, u32[]{:S(2)}) collective-permute-start(bf16[128,512]{1,0:T(8,128)(2,1)S(1)} %get-tuple-element.39), channel_id=1, source_target_pairs={{0,24},{4,28},{8,16},{12,20},{16,8},{20,12},{24,0},{28,4},{1,25},{... | collective-permute-start | bytes 393224 | tf_op jit(solution)/shard_map/ppermute | solution.py:349
  33.5 1.0 copy-start.5
  35.5 16.7 %collective-permute-start.17 = (bf16[128,512]{1,0:T(8,128)(2,1)S(1)}, bf16[128,512]{1,0:T(8,128)(2,1)S(1)}, u32[]{:S(2)}, u32[]{:S(2)}) collective-permute-start(bf16[128,512]{1,0:T(8,128)(2,1)S(1)} %get-tuple-element.50), channel_id=1, source_target_pairs={{0,20},{4,16},{8,28},{12,24},{16,4},{20,0},{24,12},{28,8},{1,21},{... | collective-permute-start | bytes 393224 | tf_op jit(solution)/shard_map/ppermute | solution.py:349
  39.3 13.2 %collective-permute-start.18 = (bf16[128,512]{1,0:T(8,128)(2,1)S(1)}, bf16[128,512]{1,0:T(8,128)(2,1)S(1)}, u32[]{:S(2)}, u32[]{:S(2)}) collective-permute-start(bf16[128,512]{1,0:T(8,128)(2,1)S(1)} %get-tuple-element.51), channel_id=1, source_target_pairs={{0,24},{4,28},{8,16},{12,20},{16,8},{20,12},{24,0},{28,4},{1,25},{... | collective-permute-start | bytes 393224 | tf_op jit(solution)/shard_map/ppermute | solution.py:349
  40.6 17.7 %collective-permute-start.19 = (bf16[128,512]{1,0:T(8,128)(2,1)S(1)}, bf16[128,512]{1,0:T(8,128)(2,1)S(1)}, u32[]{:S(2)}, u32[]{:S(2)}) collective-permute-start(bf16[128,512]{1,0:T(8,128)(2,1)S(1)} %get-tuple-element.52), channel_id=1, source_target_pairs={{0,28},{4,24},{8,20},{12,16},{16,12},{20,8},{24,4},{28,0},{1,29},{... | collective-permute-start | bytes 393224 | tf_op jit(solution)/shard_map/ppermute | solution.py:349
  44.1 15.0 %collective-permute-start.13 = (bf16[128,512]{1,0:T(8,128)(2,1)S(1)}, bf16[128,512]{1,0:T(8,128)(2,1)S(1)}, u32[]{:S(2)}, u32[]{:S(2)}) collective-permute-start(bf16[128,512]{1,0:T(8,128)(2,1)S(1)} %get-tuple-element.47), channel_id=1, source_target_pairs={{0,4},{4,0},{8,12},{12,8},{16,20},{20,16},{24,28},{28,24},{1,5},{5... | collective-permute-start | bytes 393224 | tf_op jit(solution)/shard_map/ppermute | solution.py:349
  45.7 15.0 %collective-permute-start.14 = (bf16[128,512]{1,0:T(8,128)(2,1)S(1)}, bf16[128,512]{1,0:T(8,128)(2,1)S(1)}, u32[]{:S(2)}, u32[]{:S(2)}) collective-permute-start(bf16[128,512]{1,0:T(8,128)(2,1)S(1)} %get-tuple-element.48), channel_id=1, source_target_pairs={{0,8},{4,12},{8,0},{12,4},{16,24},{20,28},{24,16},{28,20},{1,9},{5... | collective-permute-start | bytes 393224 | tf_op jit(solution)/shard_map/ppermute | solution.py:349
  52.2 16.2 %collective-permute-start.15 = (bf16[128,512]{1,0:T(8,128)(2,1)S(1)}, bf16[128,512]{1,0:T(8,128)(2,1)S(1)}, u32[]{:S(2)}, u32[]{:S(2)}) collective-permute-start(bf16[128,512]{1,0:T(8,128)(2,1)S(1)} %get-tuple-element.49), channel_id=1, source_target_pairs={{0,12},{4,8},{8,4},{12,0},{16,28},{20,24},{24,20},{28,16},{1,13},{... | collective-permute-start | bytes 393224 | tf_op jit(solution)/shard_map/ppermute | solution.py:349
  52.4 17.5 %collective-permute-start.16 = (bf16[128,512]{1,0:T(8,128)(2,1)S(1)}, bf16[128,512]{1,0:T(8,128)(2,1)S(1)}, u32[]{:S(2)}, u32[]{:S(2)}) collective-permute-start(bf16[128,512]{1,0:T(8,128)(2,1)S(1)} %get-tuple-element.45.rest_6_), channel_id=1, source_target_pairs={{0,16},{4,20},{8,24},{12,28},{16,0},{20,4},{24,8},{28,12},{1,17},{... | collective-permute-start | bytes 393224 | tf_op jit(solution)/shard_map/ppermute | solution.py:349
  58.3 12.4 %collective-permute-start.9 = (bf16[128,512]{1,0:T(8,128)(2,1)S(1)}, bf16[128,512]{1,0:T(8,128)(2,1)S(1)}, u32[]{:S(2)}, u32[]{:S(2)}) collective-permute-start(bf16[128,512]{1,0:T(8,128)(2,1)S(1)} %get-tuple-element.40), channel_id=1, source_target_pairs={{0,28},{4,24},{8,20},{12,16},{16,12},{20,8},{24,4},{28,0},{1,29},{... | collective-permute-start | bytes 393224 | tf_op jit(solution)/shard_map/ppermute | solution.py:349
  59.1 11.6 %collective-permute-start.3 = (bf16[128,512]{1,0:T(8,128)(2,1)S(1)}, bf16[128,512]{1,0:T(8,128)(2,1)S(1)}, u32[]{:S(2)}, u32[]{:S(2)}) collective-permute-start(bf16[128,512]{1,0:T(8,128)(2,1)S(1)} %get-tuple-element.35), channel_id=1, source_target_pairs={{0,4},{4,0},{8,12},{12,8},{16,20},{20,16},{24,28},{28,24},{1,5},{5... | collective-permute-start | bytes 393224 | tf_op jit(solution)/shard_map/ppermute | solution.py:349
  60.6 11.7 %collective-permute-start.4 = (bf16[128,512]{1,0:T(8,128)(2,1)S(1)}, bf16[128,512]{1,0:T(8,128)(2,1)S(1)}, u32[]{:S(2)}, u32[]{:S(2)}) collective-permute-start(bf16[128,512]{1,0:T(8,128)(2,1)S(1)} %get-tuple-element.36), channel_id=1, source_target_pairs={{0,8},{4,12},{8,0},{12,4},{16,24},{20,28},{24,16},{28,20},{1,9},{5... | collective-permute-start | bytes 393224 | tf_op jit(solution)/shard_map/ppermute | solution.py:349
  68.4 10.1 %collective-permute-start.5 = (bf16[128,512]{1,0:T(8,128)(2,1)S(1)}, bf16[128,512]{1,0:T(8,128)(2,1)S(1)}, u32[]{:S(2)}, u32[]{:S(2)}) collective-permute-start(bf16[128,512]{1,0:T(8,128)(2,1)S(1)} %get-tuple-element.37), channel_id=1, source_target_pairs={{0,12},{4,8},{8,4},{12,0},{16,28},{20,24},{24,20},{28,16},{1,13},{... | collective-permute-start | bytes 393224 | tf_op jit(solution)/shard_map/ppermute | solution.py:349
  69.9 8.6 %collective-permute-start.6 = (bf16[128,512]{1,0:T(8,128)(2,1)S(1)}, bf16[128,512]{1,0:T(8,128)(2,1)S(1)}, u32[]{:S(2)}, u32[]{:S(2)}) collective-permute-start(bf16[128,512]{1,0:T(8,128)(2,1)S(1)} %get-tuple-element.33.rest_6_), channel_id=1, source_target_pairs={{0,16},{4,20},{8,24},{12,28},{16,0},{20,4},{24,8},{28,12},{1,17},{... | collective-permute-start | bytes 393224 | tf_op jit(solution)/shard_map/ppermute | solution.py:349
  70.6 26.4 %copy-start.6 = (s32[256]{0:T(256)S(1)}, s32[256]{0:T(256)}, u32[]{:S(2)}) copy-start(s32[256]{0:T(256)} %param.15) | copy-start | bytes 3076
  94.4 13.2 %all-to-all-start.1 = ((bf16[32,32,128]{2,1,0:T(8,128)(2,1)}), bf16[32,32,128]{2,1,0:T(8,128)(2,1)S(1)}, u32[]{:S(2)}, u32[]{:S(2)}) async-start(bf16[32,32,128]{2,1,0:T(8,128)(2,1)} %broadcast_in_dim.2), calls=%async_computation.1 | async-start | bytes 524288 | tf_op jit(solution)/shard_map/all_to_all | solution.py:360

commit v3 on v2

--- a/solution.py
+++ b/solution.py
@@ -122,8 +122,8 @@
         for p in range(GROUP):
             o, e = chosen[p]
             prod[p * planes : (p + 1) * planes, :] = (
-                occ[o, :, lanes].astype(F32) * emp[e, :, lanes].astype(F32)
-            ).astype(BF16)
+                occ[o, :, lanes] * emp[e, :, lanes]
+            )
         if g == 0:
             mats[0].wait()
         along = jnp.dot(prod[...], zmat[...], preferred_element_type=F32).astype(BF16)

time: 123 us -> 123 us (level)
  no operation moved by 1% of the time
where the time goes in v3:
time: 123 us
  starting transfers between devices  38.5 us (31%)
  Pallas kernels  34.6 us (28%)
  waiting for transfers between devices  32.9 us (27%)
  blocking collectives  14.4 us (12%)
  local copies, waits for them, and re-layouts  1.72 us (1%)
    ppermute x20, starting transfers between devices, exchange(): lax.ppermute(blocks[s], axis, [(i, i ^ s) for i in range(len(blocks))])  35.9 us
    ppermute x20, waiting for transfers between devices, exchange(): lax.ppermute(blocks[s], axis, [(i, i ^ s) for i in range(len(blocks))])  23.3 us
    pallas_call x1, Pallas kernels, respond(): pl.pallas_call(functools.partial(respond_kernel, blocks, slabs, groups, f...  15 us
    all_to_all x1, blocking collectives, sum_shares(): taken = lax.all_to_all(shares, both, 0, 0, tiled=True)  14.4 us
    pallas_call x2, Pallas kernels, front(): pl.pallas_call(functools.partial(front_kernel, start, slabs, widths), out...  13.2 us
    all_to_all x1, waiting for transfers between devices, sum_shares(): return lax.all_to_all(spread, both, 0, 0, tiled=True)  9.66 us
    pallas_call x4, Pallas kernels, across(): pl.pallas_call(functools.partial(across_kernel, slabs, blocks, first, gri...  4.24 us
    all_to_all x1, starting transfers between devices, sum_shares(): return lax.all_to_all(spread, both, 0, 0, tiled=True)  2.59 us
  transfers between devices with their start and end apart: 21, of which 6 were waited for; matrix products, arithmetic and copies ran while one was open for 0% of the time, Pallas kernels for 10%

profile of v3, /device:TPU:0, one launch (start us, length us, event | category | flops | bytes accessed | tf_op | source)
XLA Modules:
  0.0 122.6 jit_solution(7818548498767105566)
XLA Ops:
  0.0 6.7 %front.2 = (bf16[256,512]{1,0:T(8,128)(2,1)}, bf16[256,512]{1,0:T(8,128)(2,1)}, bf16[256,512]{1,0:T(8,128)(2,1)}, bf16[256,512]{1,0:T(8,128)(2,1)}) custom-call(s32[32]{0:T(128)} %occ_at.3, s32[32]{0:T(128)} %emp_at.3, bf16[8,16,4096]{2,1,0:T(8,128)(2,1)} %rest_0_.3, bf16[16,16,4096]{2,1,0:T(8,128)(2,1)} %rest_1_.3, ...), custom_call_target="tpu_custom_call" | custom-call | flops 1 | bytes 1 | tf_op jit(solution)/shard_map/front/pallas_call | solution.py:149
  6.7 0.0 copy-start.3
  6.7 0.5 collective-permute-start
  7.2 2.6 %collective-permute-start.1 = (bf16[256,512]{1,0:T(8,128)(2,1)}, bf16[256,512]{1,0:T(8,128)(2,1)S(1)}, u32[]{:S(2)}, u32[]{:S(2)}) collective-permute-start(bf16[256,512]{1,0:T(8,128)(2,1)} %get-tuple-element.31), channel_id=1, source_target_pairs={{0,2},{1,3},{2,0},{3,1},{4,6},{5,7},{6,4},{7,5},{8,10},{9,11},{10,... | collective-permute-start | bytes 786440 | tf_op jit(solution)/shard_map/ppermute | solution.py:349
  9.8 0.1 collective-permute-start.2
  9.9 6.6 %front.3 = (bf16[256,512]{1,0:T(8,128)(2,1)}, bf16[256,512]{1,0:T(8,128)(2,1)}, bf16[256,512]{1,0:T(8,128)(2,1)}, bf16[256,512]{1,0:T(8,128)(2,1)}) custom-call(s32[32]{0:T(128)} %occ_at.3, s32[32]{0:T(128)} %emp_at.3, bf16[8,16,4096]{2,1,0:T(8,128)(2,1)} %rest_0_.3, bf16[16,16,4096]{2,1,0:T(8,128)(2,1)} %rest_1_.3, ...), custom_call_target="tpu_custom_call" | custom-call | flops 1 | bytes 1 | tf_op jit(solution)/shard_map/front/pallas_call | solution.py:149
  16.4 0.2 collective-permute-start.10
  16.6 1.9 %collective-permute-start.11 = (bf16[256,512]{1,0:T(8,128)(2,1)}, bf16[256,512]{1,0:T(8,128)(2,1)S(1)}, u32[]{:S(2)}, u32[]{:S(2)}) collective-permute-start(bf16[256,512]{1,0:T(8,128)(2,1)} %get-tuple-element.43), channel_id=1, source_target_pairs={{0,2},{1,3},{2,0},{3,1},{4,6},{5,7},{6,4},{7,5},{8,10},{9,11},{10,... | collective-permute-start | bytes 786440 | tf_op jit(solution)/shard_map/ppermute | solution.py:349
  18.6 0.0 collective-permute-done.rest_1_
  18.6 0.0 collective-permute-start.12
  18.6 0.0 collective-permute-done.1.rest_2_
  18.6 3.8 %collective-permute-done.2.rest_3_ = bf16[256,512]{1,0:T(8,128)(2,1)S(1)} collective-permute-done((bf16[256,512]{1,0:T(8,128)(2,1)}, bf16[256,512]{1,0:T(8,128)(2,1)S(1)}, u32[]{:S(2)}, u32[]{:S(2)}) %collective-permute-start.2) | collective-permute-done | bytes 262176 | tf_op jit(solution)/shard_map/ppermute | solution.py:349
  22.4 1.1 across.4
  23.4 3.6 %collective-permute-start.7 = (bf16[128,512]{1,0:T(8,128)(2,1)S(1)}, bf16[128,512]{1,0:T(8,128)(2,1)S(1)}, u32[]{:S(2)}, u32[]{:S(2)}) collective-permute-start(bf16[128,512]{1,0:T(8,128)(2,1)S(1)} %get-tuple-element.38), channel_id=1, source_target_pairs={{0,20},{4,16},{8,28},{12,24},{16,4},{20,0},{24,12},{28,8},{1,21},{... | collective-permute-start | bytes 393224 | tf_op jit(solution)/shard_map/ppermute | solution.py:349
  27.0 1.3 %collective-permute-start.8 = (bf16[128,512]{1,0:T(8,128)(2,1)S(1)}, bf16[128,512]{1,0:T(8,128)(2,1)S(1)}, u32[]{:S(2)}, u32[]{:S(2)}) collective-permute-start(bf16[128,512]{1,0:T(8,128)(2,1)S(1)} %get-tuple-element.39), channel_id=1, source_target_pairs={{0,24},{4,28},{8,16},{12,20},{16,8},{20,12},{24,0},{28,4},{1,25},{... | collective-permute-start | bytes 393224 | tf_op jit(solution)/shard_map/ppermute | solution.py:349
  28.4 0.0 collective-permute-done.10.rest_1_
  28.4 0.0 collective-permute-done.11.rest_2_
  28.4 5.1 %collective-permute-done.12.rest_3_ = bf16[256,512]{1,0:T(8,128)(2,1)S(1)} collective-permute-done((bf16[256,512]{1,0:T(8,128)(2,1)}, bf16[256,512]{1,0:T(8,128)(2,1)S(1)}, u32[]{:S(2)}, u32[]{:S(2)}) %collective-permute-start.12) | collective-permute-done | bytes 262176 | tf_op jit(solution)/shard_map/ppermute | solution.py:349
  33.5 0.9 copy-done.5
  34.4 1.1 across.6
  35.5 3.7 %collective-permute-start.17 = (bf16[128,512]{1,0:T(8,128)(2,1)S(1)}, bf16[128,512]{1,0:T(8,128)(2,1)S(1)}, u32[]{:S(2)}, u32[]{:S(2)}) collective-permute-start(bf16[128,512]{1,0:T(8,128)(2,1)S(1)} %get-tuple-element.50), channel_id=1, source_target_pairs={{0,20},{4,16},{8,28},{12,24},{16,4},{20,0},{24,12},{28,8},{1,21},{... | collective-permute-start | bytes 393224 | tf_op jit(solution)/shard_map/ppermute | solution.py:349
  39.2 1.3 %collective-permute-start.18 = (bf16[128,512]{1,0:T(8,128)(2,1)S(1)}, bf16[128,512]{1,0:T(8,128)(2,1)S(1)}, u32[]{:S(2)}, u32[]{:S(2)}) collective-permute-start(bf16[128,512]{1,0:T(8,128)(2,1)S(1)} %get-tuple-element.51), channel_id=1, source_target_pairs={{0,24},{4,28},{8,16},{12,20},{16,8},{20,12},{24,0},{28,4},{1,25},{... | collective-permute-start | bytes 393224 | tf_op jit(solution)/shard_map/ppermute | solution.py:349
  40.5 2.4 %collective-permute-start.19 = (bf16[128,512]{1,0:T(8,128)(2,1)S(1)}, bf16[128,512]{1,0:T(8,128)(2,1)S(1)}, u32[]{:S(2)}, u32[]{:S(2)}) collective-permute-start(bf16[128,512]{1,0:T(8,128)(2,1)S(1)} %get-tuple-element.52), channel_id=1, source_target_pairs={{0,28},{4,24},{8,20},{12,16},{16,12},{20,8},{24,4},{28,0},{1,29},{... | collective-permute-start | bytes 393224 | tf_op jit(solution)/shard_map/ppermute | solution.py:349
  43.0 1.1 across.7
  44.0 1.6 %collective-permute-start.13 = (bf16[128,512]{1,0:T(8,128)(2,1)S(1)}, bf16[128,512]{1,0:T(8,128)(2,1)S(1)}, u32[]{:S(2)}, u32[]{:S(2)}) collective-permute-start(bf16[128,512]{1,0:T(8,128)(2,1)S(1)} %get-tuple-element.47), channel_id=1, source_target_pairs={{0,4},{4,0},{8,12},{12,8},{16,20},{20,16},{24,28},{28,24},{1,5},{5... | collective-permute-start | bytes 393224 | tf_op jit(solution)/shard_map/ppermute | solution.py:349
  45.6 6.6 %collective-permute-done.17.rest_5_ = bf16[128,512]{1,0:T(8,128)(2,1)S(1)} collective-permute-done((bf16[128,512]{1,0:T(8,128)(2,1)S(1)}, bf16[128,512]{1,0:T(8,128)(2,1)S(1)}, u32[]{:S(2)}, u32[]{:S(2)}) %collective-permute-start.17) | collective-permute-done | bytes 131104 | tf_op jit(solution)/shard_map/ppermute | solution.py:349
  52.2 0.2 collective-permute-start.15
  52.3 4.8 %collective-permute-start.16 = (bf16[128,512]{1,0:T(8,128)(2,1)S(1)}, bf16[128,512]{1,0:T(8,128)(2,1)S(1)}, u32[]{:S(2)}, u32[]{:S(2)}) collective-permute-start(bf16[128,512]{1,0:T(8,128)(2,1)S(1)} %get-tuple-element.45.rest_6_), channel_id=1, source_target_pairs={{0,16},{4,20},{8,24},{12,28},{16,0},{20,4},{24,8},{28,12},{1,17},{... | collective-permute-start | bytes 393224 | tf_op jit(solution)/shard_map/ppermute | solution.py:349
  57.1 1.1 across.5
  58.2 0.9 collective-permute-start.9
  59.1 1.5 %collective-permute-start.3 = (bf16[128,512]{1,0:T(8,128)(2,1)S(1)}, bf16[128,512]{1,0:T(8,128)(2,1)S(1)}, u32[]{:S(2)}, u32[]{:S(2)}) collective-permute-start(bf16[128,512]{1,0:T(8,128)(2,1)S(1)} %get-tuple-element.35), channel_id=1, source_target_pairs={{0,4},{4,0},{8,12},{12,8},{16,20},{20,16},{24,28},{28,24},{1,5},{5... | collective-permute-start | bytes 393224 | tf_op jit(solution)/shard_map/ppermute | solution.py:349
  60.6 7.8 %collective-permute-start.4 = (bf16[128,512]{1,0:T(8,128)(2,1)S(1)}, bf16[128,512]{1,0:T(8,128)(2,1)S(1)}, u32[]{:S(2)}, u32[]{:S(2)}) collective-permute-start(bf16[128,512]{1,0:T(8,128)(2,1)S(1)} %get-tuple-element.36), channel_id=1, source_target_pairs={{0,8},{4,12},{8,0},{12,4},{16,24},{20,28},{24,16},{28,20},{1,9},{5... | collective-permute-start | bytes 393224 | tf_op jit(solution)/shard_map/ppermute | solution.py:349
  68.4 1.5 %collective-permute-start.5 = (bf16[128,512]{1,0:T(8,128)(2,1)S(1)}, bf16[128,512]{1,0:T(8,128)(2,1)S(1)}, u32[]{:S(2)}, u32[]{:S(2)}) collective-permute-start(bf16[128,512]{1,0:T(8,128)(2,1)S(1)} %get-tuple-element.37), channel_id=1, source_target_pairs={{0,12},{4,8},{8,4},{12,0},{16,28},{20,24},{24,20},{28,16},{1,13},{... | collective-permute-start | bytes 393224 | tf_op jit(solution)/shard_map/ppermute | solution.py:349
  69.8 0.0 collective-permute-start.6
  69.9 0.7 project.2.rest_8_
  70.6 0.0 copy-start.6
  70.6 1.7 %collective-permute-done.4.rest_2_ = bf16[128,512]{1,0:T(8,128)(2,1)S(1)} collective-permute-done((bf16[128,512]{1,0:T(8,128)(2,1)S(1)}, bf16[128,512]{1,0:T(8,128)(2,1)S(1)}, u32[]{:S(2)}, u32[]{:S(2)}) %collective-permute-start.4) | collective-permute-done | bytes 131104 | tf_op jit(solution)/shard_map/ppermute | solution.py:349
  72.3 6.2 %collective-permute-done.5.rest_3_ = bf16[128,512]{1,0:T(8,128)(2,1)S(1)} collective-permute-done((bf16[128,512]{1,0:T(8,128)(2,1)S(1)}, bf16[128,512]{1,0:T(8,128)(2,1)S(1)}, u32[]{:S(2)}, u32[]{:S(2)}) %collective-permute-start.5) | collective-permute-done | bytes 131104 | tf_op jit(solution)/shard_map/ppermute | solution.py:349
  78.4 0.7 project.3
  79.2 14.4 %all_to_all.10 = bf16[32,32,128]{2,1,0:T(8,128)(2,1)S(1)} all-to-all(bf16[32,32,128]{2,1,0:T(8,128)(2,1)S(1)} %project.3), channel_id=1, replica_groups=mesh['wide'=8,'narrow'=4] {'wide','narrow'}, dimensions={0} | all-to-all | bytes 524288 | tf_op jit(solution)/shard_map/all_to_all | solution.py:357
  93.6 0.1 reduce_sum.12
  93.6 0.7 broadcast_in_dim.2
  94.4 2.6 %all-to-all-start.1 = ((bf16[32,32,128]{2,1,0:T(8,128)(2,1)}), bf16[32,32,128]{2,1,0:T(8,128)(2,1)S(1)}, u32[]{:S(2)}, u32[]{:S(2)}) async-start(bf16[32,32,128]{2,1,0:T(8,128)(2,1)} %broadcast_in_dim.2), calls=%async_computation.1 | async-start | bytes 524288 | tf_op jit(solution)/shard_map/all_to_all | solution.py:360
  97.0 0.3 fusion
  97.3 0.3 turn.2.rest_2_
  97.6 0.3 turn.3.rest_3_
  97.9 9.7 %all-to-all-done.1.rest_0_ = bf16[32,32,128]{2,1,0:T(8,128)(2,1)S(1)} async-done(((bf16[32,32,128]{2,1,0:T(8,128)(2,1)}), bf16[32,32,128]{2,1,0:T(8,128)(2,1)S(1)}, u32[]{:S(2)}, u32[]{:S(2)}) %all-to-all-start.1) | async-done | bytes 262176 | tf_op jit(solution)/shard_map/all_to_all | solution.py:360
  107.6 15.0 %respond.1 = bf16[8,4096,512]{2,1,0:T(8,128)(2,1)} custom-call(bf16[32,32,128]{2,1,0:T(8,128)(2,1)S(1)} %all-to-all-done.1.rest_0_, f32[8,2,16,8]{3,2,1,0:T(8,128)S(1)} %bitcast.2, bf16[4096,128]{1,0:T(8,128)(2,1)S(1)} %turn.2.rest_2_, bf16[4096,128]{1,0:T(8,128)(2,1)S(1)} %turn.3.rest_3_), custom_call_target="tpu_custom_call" | custom-call | flops 1 | bytes 1 | tf_op jit(solution)/shard_map/respond/pallas_call | solution.py:331
  (23 shorter events, 0.1 us)
Async XLA Ops:
  0.0 97.0 %copy-start = (f32[64,8]{0,1:T(8,128)S(1)}, f32[64,8]{0,1:T(8,128)}, u32[]{:S(2)}) copy-start(f32[64,8]{0,1:T(8,128)} %param.16) | copy-start | bytes 6148
  0.0 22.3 %copy-start.2 = (bf16[4,512,256]{2,1,0:T(8,128)(2,1)S(1)}, bf16[4,512,256]{2,1,0:T(8,128)(2,1)}, u32[]{:S(2)}) copy-start(bf16[4,512,256]{2,1,0:T(8,128)(2,1)} %constant.13.clone.rest_4_) | copy-start | bytes 3145732
  0.0 22.3 %copy-start.4 = (bf16[256,256]{1,0:T(8,128)(2,1)S(1)}, bf16[256,256]{1,0:T(8,128)(2,1)}, u32[]{:S(2)}) copy-start(bf16[256,256]{1,0:T(8,128)(2,1)} %constant.14.clone.rest_5_) | copy-start | bytes 393220
  6.7 15.7 %copy-start.3 = (bf16[256,512]{1,0:T(8,128)(2,1)S(1)}, bf16[256,512]{1,0:T(8,128)(2,1)}, u32[]{:S(2)}) copy-start(bf16[256,512]{1,0:T(8,128)(2,1)} %get-tuple-element.29.rest_0_.rest_6_) | copy-start | bytes 786436
  6.7 11.9 %collective-permute-start = (bf16[256,512]{1,0:T(8,128)(2,1)}, bf16[256,512]{1,0:T(8,128)(2,1)S(1)}, u32[]{:S(2)}, u32[]{:S(2)}) collective-permute-start(bf16[256,512]{1,0:T(8,128)(2,1)} %get-tuple-element.30), channel_id=1, source_target_pairs={{0,1},{1,0},{2,3},{3,2},{4,5},{5,4},{6,7},{7,6},{8,9},{9,8},{10,11... | collective-permute-start | bytes 786440 | tf_op jit(solution)/shard_map/ppermute | solution.py:349
  7.2 11.4 %collective-permute-start.1 = (bf16[256,512]{1,0:T(8,128)(2,1)}, bf16[256,512]{1,0:T(8,128)(2,1)S(1)}, u32[]{:S(2)}, u32[]{:S(2)}) collective-permute-start(bf16[256,512]{1,0:T(8,128)(2,1)} %get-tuple-element.31), channel_id=1, source_target_pairs={{0,2},{1,3},{2,0},{3,1},{4,6},{5,7},{6,4},{7,5},{8,10},{9,11},{10,... | collective-permute-start | bytes 786440 | tf_op jit(solution)/shard_map/ppermute | solution.py:349
  9.8 12.6 %collective-permute-start.2 = (bf16[256,512]{1,0:T(8,128)(2,1)}, bf16[256,512]{1,0:T(8,128)(2,1)S(1)}, u32[]{:S(2)}, u32[]{:S(2)}) collective-permute-start(bf16[256,512]{1,0:T(8,128)(2,1)} %get-tuple-element.32), channel_id=1, source_target_pairs={{0,3},{1,2},{2,1},{3,0},{4,7},{5,6},{6,5},{7,4},{8,11},{9,10},{10,... | collective-permute-start | bytes 786440 | tf_op jit(solution)/shard_map/ppermute | solution.py:349
  16.4 12.0 %collective-permute-start.10 = (bf16[256,512]{1,0:T(8,128)(2,1)}, bf16[256,512]{1,0:T(8,128)(2,1)S(1)}, u32[]{:S(2)}, u32[]{:S(2)}) collective-permute-start(bf16[256,512]{1,0:T(8,128)(2,1)} %get-tuple-element.42), channel_id=1, source_target_pairs={{0,1},{1,0},{2,3},{3,2},{4,5},{5,4},{6,7},{7,6},{8,9},{9,8},{10,11... | collective-permute-start | bytes 786440 | tf_op jit(solution)/shard_map/ppermute | solution.py:349
  16.6 11.8 %collective-permute-start.11 = (bf16[256,512]{1,0:T(8,128)(2,1)}, bf16[256,512]{1,0:T(8,128)(2,1)S(1)}, u32[]{:S(2)}, u32[]{:S(2)}) collective-permute-start(bf16[256,512]{1,0:T(8,128)(2,1)} %get-tuple-element.43), channel_id=1, source_target_pairs={{0,2},{1,3},{2,0},{3,1},{4,6},{5,7},{6,4},{7,5},{8,10},{9,11},{10,... | collective-permute-start | bytes 786440 | tf_op jit(solution)/shard_map/ppermute | solution.py:349
  18.6 14.9 %collective-permute-start.12 = (bf16[256,512]{1,0:T(8,128)(2,1)}, bf16[256,512]{1,0:T(8,128)(2,1)S(1)}, u32[]{:S(2)}, u32[]{:S(2)}) collective-permute-start(bf16[256,512]{1,0:T(8,128)(2,1)} %get-tuple-element.44), channel_id=1, source_target_pairs={{0,3},{1,2},{2,1},{3,0},{4,7},{5,6},{6,5},{7,4},{8,11},{9,10},{10,... | collective-permute-start | bytes 786440 | tf_op jit(solution)/shard_map/ppermute | solution.py:349
  22.4 47.5 %copy-start.1 = (bf16[4096,512]{1,0:T(8,128)(2,1)S(1)}, bf16[4096,512]{1,0:T(8,128)(2,1)}, u32[]{:S(2)}) copy-start(bf16[4096,512]{1,0:T(8,128)(2,1)} %trial.3) | copy-start | bytes 12582916
  23.4 20.6 %collective-permute-start.7 = (bf16[128,512]{1,0:T(8,128)(2,1)S(1)}, bf16[128,512]{1,0:T(8,128)(2,1)S(1)}, u32[]{:S(2)}, u32[]{:S(2)}) collective-permute-start(bf16[128,512]{1,0:T(8,128)(2,1)S(1)} %get-tuple-element.38), channel_id=1, source_target_pairs={{0,20},{4,16},{8,28},{12,24},{16,4},{20,0},{24,12},{28,8},{1,21},{... | collective-permute-start | bytes 393224 | tf_op jit(solution)/shard_map/ppermute | solution.py:349
  27.0 18.6 %collective-permute-start.8 = (bf16[128,512]{1,0:T(8,128)(2,1)S(1)}, bf16[128,512]{1,0:T(8,128)(2,1)S(1)}, u32[]{:S(2)}, u32[]{:S(2)}) collective-permute-start(bf16[128,512]{1,0:T(8,128)(2,1)S(1)} %get-tuple-element.39), channel_id=1, source_target_pairs={{0,24},{4,28},{8,16},{12,20},{16,8},{20,12},{24,0},{28,4},{1,25},{... | collective-permute-start | bytes 393224 | tf_op jit(solution)/shard_map/ppermute | solution.py:349
  33.5 1.0 copy-start.5
  35.5 16.7 %collective-permute-start.17 = (bf16[128,512]{1,0:T(8,128)(2,1)S(1)}, bf16[128,512]{1,0:T(8,128)(2,1)S(1)}, u32[]{:S(2)}, u32[]{:S(2)}) collective-permute-start(bf16[128,512]{1,0:T(8,128)(2,1)S(1)} %get-tuple-element.50), channel_id=1, source_target_pairs={{0,20},{4,16},{8,28},{12,24},{16,4},{20,0},{24,12},{28,8},{1,21},{... | collective-permute-start | bytes 393224 | tf_op jit(solution)/shard_map/ppermute | solution.py:349
  39.2 13.2 %collective-permute-start.18 = (bf16[128,512]{1,0:T(8,128)(2,1)S(1)}, bf16[128,512]{1,0:T(8,128)(2,1)S(1)}, u32[]{:S(2)}, u32[]{:S(2)}) collective-permute-start(bf16[128,512]{1,0:T(8,128)(2,1)S(1)} %get-tuple-element.51), channel_id=1, source_target_pairs={{0,24},{4,28},{8,16},{12,20},{16,8},{20,12},{24,0},{28,4},{1,25},{... | collective-permute-start | bytes 393224 | tf_op jit(solution)/shard_map/ppermute | solution.py:349
  40.5 17.7 %collective-permute-start.19 = (bf16[128,512]{1,0:T(8,128)(2,1)S(1)}, bf16[128,512]{1,0:T(8,128)(2,1)S(1)}, u32[]{:S(2)}, u32[]{:S(2)}) collective-permute-start(bf16[128,512]{1,0:T(8,128)(2,1)S(1)} %get-tuple-element.52), channel_id=1, source_target_pairs={{0,28},{4,24},{8,20},{12,16},{16,12},{20,8},{24,4},{28,0},{1,29},{... | collective-permute-start | bytes 393224 | tf_op jit(solution)/shard_map/ppermute | solution.py:349
  44.0 15.0 %collective-permute-start.13 = (bf16[128,512]{1,0:T(8,128)(2,1)S(1)}, bf16[128,512]{1,0:T(8,128)(2,1)S(1)}, u32[]{:S(2)}, u32[]{:S(2)}) collective-permute-start(bf16[128,512]{1,0:T(8,128)(2,1)S(1)} %get-tuple-element.47), channel_id=1, source_target_pairs={{0,4},{4,0},{8,12},{12,8},{16,20},{20,16},{24,28},{28,24},{1,5},{5... | collective-permute-start | bytes 393224 | tf_op jit(solution)/shard_map/ppermute | solution.py:349
  45.6 15.0 %collective-permute-start.14 = (bf16[128,512]{1,0:T(8,128)(2,1)S(1)}, bf16[128,512]{1,0:T(8,128)(2,1)S(1)}, u32[]{:S(2)}, u32[]{:S(2)}) collective-permute-start(bf16[128,512]{1,0:T(8,128)(2,1)S(1)} %get-tuple-element.48), channel_id=1, source_target_pairs={{0,8},{4,12},{8,0},{12,4},{16,24},{20,28},{24,16},{28,20},{1,9},{5... | collective-permute-start | bytes 393224 | tf_op jit(solution)/shard_map/ppermute | solution.py:349
  52.2 16.2 %collective-permute-start.15 = (bf16[128,512]{1,0:T(8,128)(2,1)S(1)}, bf16[128,512]{1,0:T(8,128)(2,1)S(1)}, u32[]{:S(2)}, u32[]{:S(2)}) collective-permute-start(bf16[128,512]{1,0:T(8,128)(2,1)S(1)} %get-tuple-element.49), channel_id=1, source_target_pairs={{0,12},{4,8},{8,4},{12,0},{16,28},{20,24},{24,20},{28,16},{1,13},{... | collective-permute-start | bytes 393224 | tf_op jit(solution)/shard_map/ppermute | solution.py:349
  52.3 17.5 %collective-permute-start.16 = (bf16[128,512]{1,0:T(8,128)(2,1)S(1)}, bf16[128,512]{1,0:T(8,128)(2,1)S(1)}, u32[]{:S(2)}, u32[]{:S(2)}) collective-permute-start(bf16[128,512]{1,0:T(8,128)(2,1)S(1)} %get-tuple-element.45.rest_6_), channel_id=1, source_target_pairs={{0,16},{4,20},{8,24},{12,28},{16,0},{20,4},{24,8},{28,12},{1,17},{... | collective-permute-start | bytes 393224 | tf_op jit(solution)/shard_map/ppermute | solution.py:349
  58.2 12.4 %collective-permute-start.9 = (bf16[128,512]{1,0:T(8,128)(2,1)S(1)}, bf16[128,512]{1,0:T(8,128)(2,1)S(1)}, u32[]{:S(2)}, u32[]{:S(2)}) collective-permute-start(bf16[128,512]{1,0:T(8,128)(2,1)S(1)} %get-tuple-element.40), channel_id=1, source_target_pairs={{0,28},{4,24},{8,20},{12,16},{16,12},{20,8},{24,4},{28,0},{1,29},{... | collective-permute-start | bytes 393224 | tf_op jit(solution)/shard_map/ppermute | solution.py:349
  59.1 11.5 %collective-permute-start.3 = (bf16[128,512]{1,0:T(8,128)(2,1)S(1)}, bf16[128,512]{1,0:T(8,128)(2,1)S(1)}, u32[]{:S(2)}, u32[]{:S(2)}) collective-permute-start(bf16[128,512]{1,0:T(8,128)(2,1)S(1)} %get-tuple-element.35), channel_id=1, source_target_pairs={{0,4},{4,0},{8,12},{12,8},{16,20},{20,16},{24,28},{28,24},{1,5},{5... | collective-permute-start | bytes 393224 | tf_op jit(solution)/shard_map/ppermute | solution.py:349
  60.6 11.7 %collective-permute-start.4 = (bf16[128,512]{1,0:T(8,128)(2,1)S(1)}, bf16[128,512]{1,0:T(8,128)(2,1)S(1)}, u32[]{:S(2)}, u32[]{:S(2)}) collective-permute-start(bf16[128,512]{1,0:T(8,128)(2,1)S(1)} %get-tuple-element.36), channel_id=1, source_target_pairs={{0,8},{4,12},{8,0},{12,4},{16,24},{20,28},{24,16},{28,20},{1,9},{5... | collective-permute-start | bytes 393224 | tf_op jit(solution)/shard_map/ppermute | solution.py:349
  68.4 10.1 %collective-permute-start.5 = (bf16[128,512]{1,0:T(8,128)(2,1)S(1)}, bf16[128,512]{1,0:T(8,128)(2,1)S(1)}, u32[]{:S(2)}, u32[]{:S(2)}) collective-permute-start(bf16[128,512]{1,0:T(8,128)(2,1)S(1)} %get-tuple-element.37), channel_id=1, source_target_pairs={{0,12},{4,8},{8,4},{12,0},{16,28},{20,24},{24,20},{28,16},{1,13},{... | collective-permute-start | bytes 393224 | tf_op jit(solution)/shard_map/ppermute | solution.py:349
  69.8 8.6 %collective-permute-start.6 = (bf16[128,512]{1,0:T(8,128)(2,1)S(1)}, bf16[128,512]{1,0:T(8,128)(2,1)S(1)}, u32[]{:S(2)}, u32[]{:S(2)}) collective-permute-start(bf16[128,512]{1,0:T(8,128)(2,1)S(1)} %get-tuple-element.33.rest_6_), channel_id=1, source_target_pairs={{0,16},{4,20},{8,24},{12,28},{16,0},{20,4},{24,8},{28,12},{1,17},{... | collective-permute-start | bytes 393224 | tf_op jit(solution)/shard_map/ppermute | solution.py:349
  70.6 26.4 %copy-start.6 = (s32[256]{0:T(256)S(1)}, s32[256]{0:T(256)}, u32[]{:S(2)}) copy-start(s32[256]{0:T(256)} %param.15) | copy-start | bytes 3076
  94.4 13.2 %all-to-all-start.1 = ((bf16[32,32,128]{2,1,0:T(8,128)(2,1)}), bf16[32,32,128]{2,1,0:T(8,128)(2,1)S(1)}, u32[]{:S(2)}, u32[]{:S(2)}) async-start(bf16[32,32,128]{2,1,0:T(8,128)(2,1)} %broadcast_in_dim.2), calls=%async_computation.1 | async-start | bytes 524288 | tf_op jit(solution)/shard_map/all_to_all | solution.py:360
